TPU v7x, 128 devices: a whole 4x4x4 slice. The times are simulated.
128 devices in a mesh: dp: 32 (over y, x_hi, z), mp: 4 (over x_lo, core).
Axes of the slice: x: 4 (x_hi: 2, x_lo: 2; x = x_hi * 2 + x_lo), y: 4, z: 4, core: 2. Of those that a mesh axis runs over, the one named last changes fastest.
Arguments:
- layer_inputs: bfloat16 [4096, 1, 4096], P(('dp', 'mp')), may hold values from -6 to 6
- output_grads: bfloat16 [4096, 1, 4096], P('dp', None, 'mp'), may hold values from -0.09375 to 0.09375
- feature_order: int32 [1, 4096], replicated, may hold values from 0 to 4095, each once within a row
- block_slot: int32 [4], replicated, may hold values from 0 to 3, each once
- layer_owner: int32 [32], replicated, may hold values from 0 to 31, each once
- in_basis: float32 [4096, 1024], P('dp'), may hold values from -0.1875 to 0.1875
- in_values: float32 [4096], P('dp'), may hold values from 0.1 to 10
- out_basis: float32 [32, 4096, 1024], P('dp', 'mp'), may hold values from -0.1875 to 0.1875
- out_values: float32 [32, 4096], P('dp', 'mp'), may hold values from 0.1 to 10
Outputs:
- preconditioned: float32 [4096, 4096], P('dp', 'mp')
Inputs may be any that keep to these rules, and one draw needn't show every extreme that they name: `feature_order`: each layer's features are split into 4 blocks of 1024. `block_slot`: every slot holds exactly one input block. `layer_owner`: distinct dp indices.
All inputs are finite; a program needn't handle non-finite values.
Results may differ from a plain program's by a relative error of at most 0.0003.
Values may be sent and summed in bfloat16 or wider, within the bound.
No kernel may reach another device: no remote copies, remote signals or barrier semaphores. Data moves between devices by JAX's collectives and lax.ppermute only.
A program may use at most 128 MiB of HBM per device.

v0:
```python
import jax
import jax.numpy as jnp
from jax import lax
from jax.experimental import pallas as pl
from jax.experimental.pallas import tpu as pltpu
from jax.sharding import Mesh, PartitionSpec as P

DIN = 4096
BLK = 1024
LANES = 128
GROUP = 256
ROWS = 136
DAMPING = 0.1
TOP = 32767.0
LOG_UNIT = 65536.0
VALUE_UNIT = 134217728.0
PAIR = ("h", "z")
ALL_DP = ("y", "h", "z")
VMEM = 48 * 1024 * 1024
f32, bf16, i32 = jnp.float32, jnp.bfloat16, jnp.int32


def params(*semantics):
    return pltpu.CompilerParams(vmem_limit_bytes=VMEM, dimension_semantics=semantics or None)


def mul(a, b, ca=1, cb=0):
    return lax.dot_general(a, b, (((ca,), (cb,)), ((), ())), preferred_element_type=f32)


def halves(a):
    high = a.astype(bf16)
    return high, (a - high.astype(f32)).astype(bf16)


def gather_kernel(me_ref, order_ref, x_ref, out_ref):
    x = [x_ref[:, k * LANES:(k + 1) * LANES].astype(f32) for k in range(DIN // LANES)]
    for n in range(4):
        pair = sum(jnp.where(me_ref[4 + j] == pl.program_id(0) * 2 + n // 2, j, 0) for j in range(4))
        start = pair * BLK + n % 2 * 512
        for b in range(4):
            idx = order_ref[:, pl.ds(pl.multiple_of(start + b * LANES, LANES), LANES)]
            lane = jnp.broadcast_to(jnp.bitwise_and(idx, LANES - 1), (32, LANES))
            src = jnp.broadcast_to(jnp.right_shift(idx, 7), (32, LANES))
            acc = jnp.zeros((32, LANES), f32)
            for k in range(DIN // LANES):
                acc = jnp.where(src == k, jnp.take_along_axis(x[k], lane, axis=1), acc)
            out_ref[n, :, b * LANES:(b + 1) * LANES] = acc.astype(bf16)


def gather_columns(me, order, x):
    return pl.pallas_call(
        gather_kernel,
        grid=(2,),
        in_specs=[
            pl.BlockSpec(memory_space=pltpu.SMEM),
            pl.BlockSpec((1, DIN), lambda i: (0, 0)),
            pl.BlockSpec((32, DIN), lambda i: (0, 0)),
        ],
        out_specs=pl.BlockSpec((4, 32, 512), lambda i: (i, 0, 0)),
        out_shape=jax.ShapeDtypeStruct((8, 32, 512), bf16),
        compiler_params=params("arbitrary"),
        cost_estimate=pl.CostEstimate(flops=10**6, bytes_accessed=10**6, transcendentals=0),
    )(me, order, x)


def diagonal():
    return lax.broadcasted_iota(i32, (LANES, LANES), 0) == lax.broadcasted_iota(i32, (LANES, LANES), 1)


def encode(part):
    most = jnp.maximum(jnp.max(jnp.abs(part), axis=1, keepdims=True), 1e-30)
    code = jnp.ceil(jnp.log2(most) * LOG_UNIT) + 4.0
    q = jnp.round(part * (TOP * jnp.exp2(-code / LOG_UNIT))).astype(i32)
    word = jnp.bitwise_or(jnp.left_shift(q[:, LANES:], 16), jnp.bitwise_and(q[:, :LANES], 65535))
    return word, code.astype(i32)


def decode(word, unit):
    first = jnp.right_shift(jnp.left_shift(word, 16), 16).astype(f32) * unit
    return first, jnp.right_shift(word, 16).astype(f32) * unit


def to_row(column, eye):
    return jnp.sum(jnp.where(eye, column, 0), axis=0, keepdims=True)


def to_unit(row, eye):
    return jnp.exp2(jnp.sum(jnp.where(eye, row, 0), axis=1, keepdims=True).astype(f32) / LOG_UNIT) / TOP


def pack_kernel(basis_ref, values_ref, out_ref):
    eye = diagonal()
    blocks = values_ref.shape[1] // LANES
    count = out_ref.shape[0]
    for n in range(count // 4):
        codes = [[] for _ in range(4)]
        for g in range(4):
            word, code = encode(basis_ref[n * LANES:(n + 1) * LANES, g * GROUP:(g + 1) * GROUP])
            for d in range(4):
                out_ref[n * 4 + d, g * 32:(g + 1) * 32, :] = word[d * 32:(d + 1) * 32]
                codes[d].append(code[d * 32:(d + 1) * 32])
        for d in range(4):
            row = to_row(jnp.concatenate(codes[d], axis=0), eye)
            block = (n * 4 + d) % blocks
            coded = (values_ref[:, block * LANES:(block + 1) * LANES] * VALUE_UNIT).astype(i32)
            out_ref[n * 4 + d, LANES:ROWS, :] = jnp.concatenate([row, coded, jnp.zeros((6, LANES), i32)], axis=0)


def pack_basis(basis, values):
    rows = basis.shape[0]
    size = min(rows, 512)
    return pl.pallas_call(
        pack_kernel,
        grid=(rows // size,),
        in_specs=[pl.BlockSpec((size, BLK), lambda i: (i, 0)), pl.BlockSpec(values.shape, lambda i: (0, 0))],
        out_specs=pl.BlockSpec((size // 32, ROWS, LANES), lambda i: (i, 0, 0)),
        out_shape=jax.ShapeDtypeStruct((rows // 32, ROWS, LANES), i32),
        compiler_params=params("arbitrary"),
        cost_estimate=pl.CostEstimate(flops=rows * 10**4, bytes_accessed=rows * 6000, transcendentals=0),
    )(basis, values)


def decode_chunks(get, base, count, high_ref, low_ref, eye):
    for d in range(count):
        unit = to_unit(get(d, LANES, 1), eye)
        for g in range(4):
            pair = decode(get(d, g * 32, 32), unit[g * 32:(g + 1) * 32])
            for k in range(2):
                high, low = halves(pair[k])
                where = (pl.ds(base + d * 32, 32), slice(g * GROUP + k * LANES, g * GROUP + (k + 1) * LANES))
                high_ref[where] = high
                low_ref[where] = low


def unpack_kernel(me_ref, own_ref, other_ref, high_ref, low_ref, side_ref):
    core = lax.rem(me_ref[3], 2)
    eye = diagonal()
    for z in range(4):
        def get(d, start, size):
            rows = slice(start, start + size)
            return jnp.where(core == d // 2, own_ref[z, 0, d % 2, rows, :], other_ref[z, 0, d % 2, rows, :])
        decode_chunks(get, z * LANES, 4, high_ref, low_ref, eye)
        side_ref[z] = get(0, LANES, 8)


def unpack_basis(me, own, other):
    rows = lambda i, m: (i, 0)
    half = pl.BlockSpec((4, 1, 2, ROWS, LANES), lambda i, m: (0, lax.rem(i + m[1], 2), 0, 0, 0))
    return pl.pallas_call(
        unpack_kernel,
        grid_spec=pltpu.PrefetchScalarGridSpec(
            num_scalar_prefetch=1,
            grid=(2,),
            in_specs=[half, half],
            out_specs=[pl.BlockSpec((512, BLK), rows)] * 2 + [pl.BlockSpec((4, 8, LANES), lambda i, m: (i, 0, 0))],
        ),
        out_shape=[jax.ShapeDtypeStruct((BLK, BLK), bf16)] * 2 + [jax.ShapeDtypeStruct((8, 8, LANES), i32)],
        compiler_params=params("arbitrary"),
        cost_estimate=pl.CostEstimate(flops=10**7, bytes_accessed=6 * 10**6, transcendentals=0),
    )(me, own, other)


def partial_kernel(me_ref, x0_ref, x1_ref, x2_ref, x3_ref, grads_ref, *refs):
    own_ref, word_refs, tokens, total = refs[0], refs[1:4], refs[4], refs[5]
    for j, x_ref in enumerate((x0_ref, x1_ref, x2_ref, x3_ref)):
        place = jnp.bitwise_xor(me_ref[3], j)
        for r in range(8):
            tokens[pl.ds(pl.multiple_of(r * LANES + place * 32, 32), 32), :] = x_ref[r]
    for r in range(4):
        grads = jnp.concatenate([grads_ref[r, me_ref[1]], grads_ref[r, 1 - me_ref[1]]], axis=0)
        part = mul(tokens[r * GROUP:(r + 1) * GROUP, :], grads, 0, 0)
        total[...] = part if r == 0 else total[...] + part
    eye = diagonal()
    for k in range(4):
        start = pl.multiple_of(lax.rem(me_ref[2] + k, 4) * LANES, LANES)
        if k == 0:
            own_ref[...] = total[pl.ds(start, LANES), :]
            continue
        rows = []
        for g in range(4):
            word, code = encode(total[pl.ds(start, LANES), g * GROUP:(g + 1) * GROUP])
            word_refs[k - 1][g * LANES:(g + 1) * LANES, :] = word
            rows.append(to_row(code, eye))
        word_refs[k - 1][4 * LANES:, :] = jnp.concatenate(rows + [jnp.zeros((4, LANES), i32)], axis=0)


def partial_rows(me, tokens, grads):
    vmem = pl.BlockSpec(memory_space=pltpu.VMEM)
    return pl.pallas_call(
        partial_kernel,
        in_specs=[pl.BlockSpec(memory_space=pltpu.SMEM)] + [vmem] * 5,
        out_specs=[vmem] * 4,
        out_shape=[jax.ShapeDtypeStruct((LANES, BLK), f32)] + [jax.ShapeDtypeStruct((520, LANES), i32)] * 3,
        scratch_shapes=[pltpu.VMEM((BLK, 512), bf16), pltpu.VMEM((512, BLK), f32)],
        compiler_params=params(),
        cost_estimate=pl.CostEstimate(flops=10**9, bytes_accessed=5 * 10**6, transcendentals=0),
    )(me, *tokens, grads)


def front_kernel(got_ref, own_ref, w1_ref, w2_ref, w3_ref, v_ref, high_ref, low_ref, grad):
    step = pl.program_id(0)
    eye = diagonal()
    decode_chunks(lambda d, start, size: got_ref[d, start:start + size, :], 0, 16, high_ref, low_ref, eye)

    @pl.when(step == 0)
    def _():
        for g in range(4):
            sums = [own_ref[:, g * GROUP:g * GROUP + LANES], own_ref[:, g * GROUP + LANES:(g + 1) * GROUP]]
            for ref in (w1_ref, w2_ref, w3_ref):
                unit = to_unit(ref[4 * LANES + g:4 * LANES + g + 1, :], eye)
                pair = decode(ref[g * LANES:(g + 1) * LANES, :], unit)
                sums = [sums[0] + pair[0], sums[1] + pair[1]]
            grad[g // 2, :, g % 2 * GROUP:(g % 2 + 1) * GROUP] = jnp.concatenate(sums, axis=1)

    grad_high, grad_low = halves(grad[step])
    both = mul(jnp.concatenate([grad_high, grad_low], axis=0), high_ref[...])
    v = both[:LANES] + both[LANES:] + mul(grad_high, low_ref[...])
    for c in range(8):
        part = v[:, c * LANES:(c + 1) * LANES]
        v_ref[c] = jnp.where(step == 0, part, v_ref[c] + part)


def front(got, own, words):
    whole = lambda i: (0, 0)
    return pl.pallas_call(
        front_kernel,
        grid=(2,),
        in_specs=[pl.BlockSpec((16, ROWS, LANES), lambda i: (i, 0, 0)), pl.BlockSpec((LANES, BLK), whole)]
        + [pl.BlockSpec((520, LANES), whole)] * 3,
        out_specs=[pl.BlockSpec((8, LANES, LANES), lambda i: (0, 0, 0))]
        + [pl.BlockSpec((512, BLK), lambda i: (i, 0))] * 2,
        out_shape=[jax.ShapeDtypeStruct((8, LANES, LANES), f32)] + [jax.ShapeDtypeStruct((BLK, BLK), bf16)] * 2,
        scratch_shapes=[pltpu.VMEM((2, LANES, 512), f32)],
        compiler_params=params("arbitrary"),
        cost_estimate=pl.CostEstimate(flops=8 * 10**8, bytes_accessed=8 * 10**6, transcendentals=0),
    )(got, own, *words)


def middle_kernel(v_ref, high_ref, low_ref, in_side_ref, out_side_ref, u_ref):
    v = v_ref[...].reshape(BLK, LANES)
    v_high, v_low = halves(v)
    qh, ql = high_ref[...], low_ref[...]
    both = mul(jnp.concatenate([v_high, v_low], axis=1), qh, 0, 0)
    rt = both[:LANES] + both[LANES:] + mul(v_high, ql, 0, 0)
    la = jnp.concatenate([in_side_ref[c, 1:2, :] for c in range(8)], axis=1).astype(f32) / VALUE_UNIT
    lb = jnp.sum(jnp.where(diagonal(), out_side_ref[0, 1:2, :], 0), axis=1, keepdims=True).astype(f32) / VALUE_UNIT
    st = rt / (lb * la + DAMPING)
    s_high, s_low = halves(st)
    both = mul(jnp.concatenate([s_high, s_low], axis=0), qh, 1, 1)
    ut = both[:LANES] + both[LANES:] + mul(s_high, ql, 1, 1)
    for c in range(8):
        u_ref[c] = ut[:, c * LANES:(c + 1) * LANES]


def middle(v, high, low, in_side, piece):
    whole = lambda i: (0, 0)
    return pl.pallas_call(
        middle_kernel,
        grid=(1,),
        in_specs=[
            pl.BlockSpec((8, LANES, LANES), lambda i: (0, 0, 0)),
            pl.BlockSpec((BLK, BLK), whole),
            pl.BlockSpec((BLK, BLK), whole),
            pl.BlockSpec((8, 8, LANES), lambda i: (0, 0, 0)),
            pl.BlockSpec((1, 8, LANES), lambda i: (0, 16, 0)),
        ],
        out_specs=pl.BlockSpec((8, LANES, LANES), lambda i: (0, 0, 0)),
        out_shape=jax.ShapeDtypeStruct((8, LANES, LANES), f32),
        compiler_params=params("arbitrary"),
        cost_estimate=pl.CostEstimate(flops=16 * 10**8, bytes_accessed=6 * 10**6, transcendentals=0),
    )(v, high, low, in_side, piece)


def back_kernel(u_ref, high_ref, low_ref, out_ref):
    u_high, u_low = halves(u_ref[...].reshape(BLK, LANES).T)
    both = mul(jnp.concatenate([u_high, u_low], axis=0), high_ref[...], 1, 1)
    out_ref[...] = both[:LANES] + both[LANES:] + mul(u_high, low_ref[...], 1, 1)


def back(u, high, low):
    return pl.pallas_call(
        back_kernel,
        grid=(2,),
        in_specs=[
            pl.BlockSpec((8, LANES, LANES), lambda i: (0, 0, 0)),
            pl.BlockSpec((512, BLK), lambda i: (i, 0)),
            pl.BlockSpec((512, BLK), lambda i: (i, 0)),
        ],
        out_specs=pl.BlockSpec((LANES, 512), lambda i: (0, i)),
        out_shape=jax.ShapeDtypeStruct((LANES, BLK), f32),
        compiler_params=params("arbitrary"),
        cost_estimate=pl.CostEstimate(flops=8 * 10**8, bytes_accessed=5 * 10**6, transcendentals=0),
    )(u, high, low)


def body(
    layer_inputs,
    output_grads,
    feature_order,
    block_slot,
    layer_owner,
    in_basis,
    in_values,
    out_basis,
    out_values,
):
    me = jnp.stack([lax.axis_index("y"), lax.axis_index("h"), lax.axis_index("z"), lax.axis_index(("l", "c"))])
    me = jnp.concatenate([me.astype(i32), block_slot])

    in_part = pack_basis(in_basis, in_values.reshape(1, LANES))
    in_part = lax.dynamic_slice_in_dim(in_part, lax.axis_index("c") * 2, 2, 0)
    in_pair = jnp.stack([in_part, lax.ppermute(in_part, ("h", "l"), [(i, 3 - i) for i in range(4)])])

    chunks = gather_columns(me, feature_order, layer_inputs.reshape(32, DIN))
    grads = output_grads.reshape(LANES, BLK)
    grads = jnp.stack([grads, flip(grads, "h")])
    chunks, grads, out_part = lax.optimization_barrier((chunks, grads, out_basis[0]))
    moved = lax.all_to_all(chunks, ("y", "h"), 0, 0, tiled=True)
    tokens = [moved] + [lax.ppermute(moved, ("l", "c"), [(m, m ^ j) for m in range(4)]) for j in range(1, 4)]

    packed = pack_basis(out_part, out_values)
    packed, in_pair, *tokens = lax.optimization_barrier((packed, in_pair, *tokens))
    spread = lax.all_to_all(packed, ALL_DP, 0, 0, tiled=True)
    piece = lax.dynamic_index_in_dim(spread, layer_owner[0], 0, keepdims=True)

    grads = lax.all_gather(grads, "y")
    _, in_pair = lax.optimization_barrier((grads, in_pair))
    in_all = lax.all_gather(in_pair, "z")
    own, *words = partial_rows(me, tokens, grads)
    words = [along(w, "z", k + 1) for k, w in enumerate(words)]
    piece, words = lax.optimization_barrier((piece, words))

    got = lax.all_to_all(jnp.broadcast_to(piece, spread.shape), ALL_DP, 0, 0, tiled=True)
    v, out_high, out_low = front(got, own, words)

    v = lax.all_to_all(v, PAIR, 0, 0, tiled=True)
    in_high, in_low, in_side = unpack_basis(me, in_all, jnp.stack([flip(in_all[z], "c") for z in range(4)]))
    u = middle(v, in_high, in_low, in_side, piece)
    u = lax.all_to_all(u, PAIR, 0, 0, tiled=True)
    return back(u, out_high, out_low)


def along(block, axis, shift):
    if shift == 0:
        return block
    return lax.ppermute(block, axis, [(i, (i + shift) % 4) for i in range(4)])


def flip(block, axis):
    return lax.ppermute(block, axis, [(0, 1), (1, 0)])


def solution(mesh):
    fine = Mesh(mesh.devices.reshape(4, 2, 4, 2, 2), ("y", "h", "z", "l", "c"))
    dp, mp = ("y", "h", "z"), ("l", "c")
    in_specs = (
        P(dp + mp, None, None),
        P(dp, None, mp),
        P(),
        P(),
        P(),
        P(dp, None),
        P(dp),
        P(dp, mp, None),
        P(dp, mp),
    )
    return jax.shard_map(body, mesh=fine, in_specs=in_specs, out_specs=P(dp, mp), check_vma=False)
```

profile of v0, /device:TPU:0, one launch (start us, length us, event | category | flops | bytes accessed | tf_op | source)
XLA Modules:
  0.0 191.9 jit_solution(12560730246707971224)
XLA Ops:
  6.5 3.1 %collective-permute-start = (bf16[128,1024]{1,0:T(8,128)(2,1)}, bf16[128,1024]{1,0:T(8,128)(2,1)S(1)}, u32[]{:S(2)}, u32[]{:S(2)}) collective-permute-start(bf16[128,1024]{1,0:T(8,128)(2,1)} %bitcast.32), channel_id=1, source_target_pairs={{0,16},{16,0},{1,17},{17,1},{2,18},{18,2},{3,19},{19,3},{4,20},{20... | collective-permute-start | bytes 786440 | tf_op jit(solution)/shard_map/ppermute | solution.py:351
  9.6 0.7 concatenate.3.me_ref
  10.4 0.9 copy-done.4
  11.3 0.7 copy-done.5
  12.1 3.6 %shard_map.91 = bf16[8,32,512]{2,1,0:T(8,128)(2,1)} custom-call(s32[8]{0:T(128)S(1)} %concatenate.3.me_ref, s32[1,4096]{1,0:T(1,128)S(1)} %copy-done.5, bf16[32,4096]{1,0:T(8,128)(2,1)S(1)} %bitcast.24), custom_call_target="tpu_custom_call" | custom-call | flops 1000000 | bytes 1000000 | tf_op jit(solution)/shard_map/pallas_call | solution.py:52
  15.7 0.5 collective-permute-done
  16.2 1.8 pad_maximum_fusion
  18.0 7.2 %all-to-all-start = ((bf16[8,32,512]{2,1,0:T(8,128)(2,1)}), bf16[8,32,512]{2,1,0:T(8,128)(2,1)S(1)}, u32[]{:S(2)}, u32[]{:S(2)}) async-start(bf16[8,32,512]{2,1,0:T(8,128)(2,1)} %shard_map.91), calls=%async_computation | async-start | bytes 524288 | tf_op jit(solution)/shard_map/all_to_all | solution.py:319
  25.2 0.4 shard_map.93
  25.5 8.4 %all-to-all-done.x0_ref = bf16[8,32,512]{2,1,0:T(8,128)(2,1)S(1)} async-done(((bf16[8,32,512]{2,1,0:T(8,128)(2,1)}), bf16[8,32,512]{2,1,0:T(8,128)(2,1)S(1)}, u32[]{:S(2)}, u32[]{:S(2)}) %all-to-all-start) | async-done | bytes 262176 | tf_op jit(solution)/shard_map/all_to_all | solution.py:319
  33.9 0.6 collective-permute-start.3
  34.5 1.3 collective-permute-start.4
  35.8 0.7 collective-permute-start.1
  36.5 6.5 %collective-permute-done.1 = s32[2,136,128]{2,1,0:T(8,128)S(1)} collective-permute-done((s32[2,136,128]{2,1,0:T(8,128)S(1)}, s32[2,136,128]{2,1,0:T(8,128)S(1)}, u32[]{:S(2)}, u32[]{:S(2)}) %collective-permute-start.1) | collective-permute-done | bytes 139296 | tf_op jit(solution)/shard_map/ppermute | solution.py:313
  43.0 0.7 pad_add_fusion.1
  43.7 4.6 %shard_map.92 = s32[32,136,128]{2,1,0:T(8,128)} custom-call(f32[1024,1024]{1,0:T(8,128)} %bitcast.27, f32[1,1024]{1,0:T(1,128)S(1)} %copy-done.6), custom_call_target="tpu_custom_call" | custom-call | flops 10240000 | bytes 6144000 | tf_op jit(solution)/shard_map/pallas_call | solution.py:113
  48.3 6.4 %all-to-all-start.1 = ((s32[32,136,128]{2,1,0:T(8,128)}), s32[32,136,128]{2,1,0:T(8,128)}, u32[]{:S(2)}, u32[]{:S(2)}) async-start(s32[32,136,128]{2,1,0:T(8,128)} %shard_map.92), calls=%async_computation.1 | async-start | bytes 4456448 | tf_op jit(solution)/shard_map/all_to_all | solution.py:324
  54.7 1.6 copy-done.8
  56.3 2.6 %shard_map.94 = (f32[128,1024]{1,0:T(8,128)S(1)}, s32[520,128]{1,0:T(8,128)S(1)}, s32[520,128]{1,0:T(8,128)S(1)}, s32[520,128]{1,0:T(8,128)S(1)}) custom-call(s32[8]{0:T(128)S(1)} %concatenate.3.me_ref, bf16[8,32,512]{2,1,0:T(8,128)(2,1)S(1)} %all-to-all-done.x0_ref, bf16[8,32,512]{2,1,0:T(8,128)(2,1)S(1)} %collective-permute-done.2.x1_ref, ...), custom_call_target="tpu_custom_call" | custom-call | flops 1000000000 | bytes 5000000 | tf_op jit(solution)/shard_map/pallas_call | solution.py:190
  58.9 1.8 collective-permute-start.5
  60.7 2.7 %collective-permute-start.6 = (s32[520,128]{1,0:T(8,128)S(1)}, s32[520,128]{1,0:T(8,128)S(1)}, u32[]{:S(2)}, u32[]{:S(2)}) collective-permute-start(s32[520,128]{1,0:T(8,128)S(1)} %get-tuple-element.38), channel_id=1, source_target_pairs={{0,8},{4,12},{8,0},{12,4},{1,9},{5,13},{9,1},{13,5},{2,10},{6,14},... | collective-permute-start | bytes 798728 | tf_op jit(solution)/shard_map/ppermute | solution.py:347
  63.3 1.5 collective-permute-start.7
  64.9 21.8 %all-to-all-done.1 = s32[32,136,128]{2,1,0:T(8,128)} async-done(((s32[32,136,128]{2,1,0:T(8,128)}), s32[32,136,128]{2,1,0:T(8,128)}, u32[]{:S(2)}, u32[]{:S(2)}) %all-to-all-start.1) | async-done | bytes 2228256 | tf_op jit(solution)/shard_map/all_to_all | solution.py:324
  86.7 0.9 constant_dynamic-slice_fusion.out_side_ref
  87.6 7.5 %collective-permute-done.5.w1_ref = s32[520,128]{1,0:T(8,128)S(1)} collective-permute-done((s32[520,128]{1,0:T(8,128)S(1)}, s32[520,128]{1,0:T(8,128)S(1)}, u32[]{:S(2)}, u32[]{:S(2)}) %collective-permute-start.5) | collective-permute-done | bytes 266272 | tf_op jit(solution)/shard_map/ppermute | solution.py:347
  95.0 2.9 %collective-permute-done.7.w3_ref = s32[520,128]{1,0:T(8,128)S(1)} collective-permute-done((s32[520,128]{1,0:T(8,128)S(1)}, s32[520,128]{1,0:T(8,128)S(1)}, u32[]{:S(2)}, u32[]{:S(2)}) %collective-permute-start.7) | collective-permute-done | bytes 266272 | tf_op jit(solution)/shard_map/ppermute | solution.py:347
  97.9 1.5 broadcast_in_dim.8
  99.5 5.5 %all-to-all-start.2 = ((s32[32,136,128]{2,1,0:T(8,128)}), s32[32,136,128]{2,1,0:T(8,128)}, u32[]{:S(2)}, u32[]{:S(2)}) async-start(s32[32,136,128]{2,1,0:T(8,128)} %broadcast_in_dim.8), calls=%async_computation.2 | async-start | bytes 4456448 | tf_op jit(solution)/shard_map/all_to_all | solution.py:334
  105.0 0.7 all-gather.7.cloned.1.call-update
  105.7 30.0 %all-to-all-done.2.got_ref = s32[32,136,128]{2,1,0:T(8,128)} async-done(((s32[32,136,128]{2,1,0:T(8,128)}), s32[32,136,128]{2,1,0:T(8,128)}, u32[]{:S(2)}, u32[]{:S(2)}) %all-to-all-start.2) | async-done | bytes 2228256 | tf_op jit(solution)/shard_map/all_to_all | solution.py:334
  135.7 5.9 %shard_map.95 = (f32[8,128,128]{2,1,0:T(8,128)}, bf16[1024,1024]{1,0:T(8,128)(2,1)S(1)}, bf16[1024,1024]{1,0:T(8,128)(2,1)S(1)}) custom-call(s32[32,136,128]{2,1,0:T(8,128)} %all-to-all-done.2.got_ref, f32[128,1024]{1,0:T(8,128)S(1)} %get-tuple-element.41.own_ref, s32[520,128]{1,0:T(8,128)S(1)} %collective-permute-done.5.w1_ref, ...), custom_call_target="tpu_custom_call" | custom-call | flops 800000000 | bytes 8000000 | tf_op jit(solution)/shard_map/pallas_call | solution.py:226
  141.6 1.4 copy-done.1
  142.9 5.9 %all-to-all-start.3 = ((f32[8,128,128]{2,1,0:T(8,128)}), f32[8,128,128]{2,1,0:T(8,128)S(1)}, u32[]{:S(2)}, u32[]{:S(2)}) async-start(f32[8,128,128]{2,1,0:T(8,128)} %get-tuple-element.45), calls=%async_computation.3 | async-start | bytes 1048576 | tf_op jit(solution)/shard_map/all_to_all | solution.py:337
  148.9 1.4 fusion
  150.4 0.5 collective-permute-start.10
  151.0 0.4 collective-permute-start.8
  151.4 0.5 collective-permute-done.11
  151.9 0.4 collective-permute-done.10
  152.3 0.4 collective-permute-done.9
  152.7 0.4 collective-permute-done.8
  153.2 3.9 %shard_map.96 = (bf16[1024,1024]{1,0:T(8,128)(2,1)S(1)}, bf16[1024,1024]{1,0:T(8,128)(2,1)}, s32[8,8,128]{2,1,0:T(8,128)S(1)}) custom-call(s32[8]{0:T(128)S(1)} %concatenate.3.me_ref, s32[4,2,2,136,128]{4,3,2,1,0:T(8,128)S(1)} %bitcast.22, s32[4,2,2,136,128]{4,3,2,1,0:T(8,128)S(1)} %pad_add_fusion.other_ref), custom_call_target="tpu_custom_call" | custom-call | flops 10000000 | bytes 6000000 | tf_op jit(solution)/shard_map/pallas_call | solution.py:150
  157.1 1.4 copy-done.9
  158.5 0.2 all-to-all-done.3.v_ref
  158.7 1.6 copy-done.10
  160.2 1.6 copy-done.11
  161.8 2.3 %shard_map.97 = f32[8,128,128]{2,1,0:T(8,128)S(1)} custom-call(f32[8,128,128]{2,1,0:T(8,128)S(1)} %all-to-all-done.3.v_ref, bf16[1024,1024]{1,0:T(8,128)(2,1)S(1)} %copy-done.10, bf16[1024,1024]{1,0:T(8,128)(2,1)S(1)} %copy-done.11, s32[8,8,128]{2,1,0:T(8,128)S(1)} %get-tuple-element.50.in_side_ref, s32[1,136,128]{2,1,0:T(8,128)S(1)} %constant_dynamic-slice_fusion.out_side_ref), custom_call_target="tpu_custom_call" | custom-call | flops 1600000000 | bytes 6000000 | tf_op jit(solution)/shard_map/pallas_call | solution.py:258
  164.1 18.7 %all_to_all.25.u_ref = f32[8,128,128]{2,1,0:T(8,128)S(1)} all-to-all(f32[8,128,128]{2,1,0:T(8,128)S(1)} %shard_map.97), channel_id=1, replica_groups=mesh['y'=4,'h'=2,'z'=4,'l'=2,'c'=2] {'h','z'}, dimensions={0} | all-to-all | bytes 1048576 | tf_op jit(solution)/shard_map/all_to_all | solution.py:340
  182.8 2.3 %shard_map.98 = f32[128,1024]{1,0:T(8,128)} custom-call(f32[8,128,128]{2,1,0:T(8,128)S(1)} %all_to_all.25.u_ref, bf16[1024,1024]{1,0:T(8,128)(2,1)S(1)} %get-tuple-element.51.high_ref, bf16[1024,1024]{1,0:T(8,128)(2,1)S(1)} %copy-done.2), custom_call_target="tpu_custom_call" | custom-call | flops 800000000 | bytes 5000000 | tf_op jit(solution)/shard_map/pallas_call | solution.py:282
  (34 shorter events, 0.4 us)
Async XLA Ops:
  6.5 18.6 %copy-start.3 = (f32[128,1024]{1,0:T(8,128)S(1)}, f32[128,1024]{1,0:T(8,128)}, u32[]{:S(2)}) copy-start(f32[128,1024]{1,0:T(8,128)} %basis_ref.1) | copy-start | bytes 1572868
  6.5 48.2 %all-gather.5.cloned.1.call-start = ((), (), s32[]{:S(2)}) async-start(), calls=%async_computation.5 | async-start | bytes 2621440 | tf_op jit(solution)/shard_map/all_gather | solution.py:327
  6.5 9.6 %collective-permute-start = (bf16[128,1024]{1,0:T(8,128)(2,1)}, bf16[128,1024]{1,0:T(8,128)(2,1)S(1)}, u32[]{:S(2)}, u32[]{:S(2)}) collective-permute-start(bf16[128,1024]{1,0:T(8,128)(2,1)} %bitcast.32), channel_id=1, source_target_pairs={{0,16},{16,0},{1,17},{17,1},{2,18},{18,2},{3,19},{19,3},{4,20},{20... | collective-permute-start | bytes 786440 | tf_op jit(solution)/shard_map/ppermute | solution.py:351
  10.4 1.0 copy-start.4
  11.3 0.7 copy-start.5
  12.0 13.1 %copy-start.7 = (f32[128]{0:T(128)S(1)}, f32[128]{0:T(128)}, u32[]{:S(2)}) copy-start(f32[128]{0:T(128)} %param.15) | copy-start | bytes 1540
  15.7 28.0 %copy-start.6 = (f32[1,1024]{1,0:T(1,128)S(1)}, f32[1,1024]{1,0:T(1,128)}, u32[]{:S(2)}) copy-start(f32[1,1024]{1,0:T(1,128)} %values_ref.1) | copy-start | bytes 12292
  18.0 16.0 %all-to-all-start = ((bf16[8,32,512]{2,1,0:T(8,128)(2,1)}), bf16[8,32,512]{2,1,0:T(8,128)(2,1)S(1)}, u32[]{:S(2)}, u32[]{:S(2)}) async-start(bf16[8,32,512]{2,1,0:T(8,128)(2,1)} %shard_map.91), calls=%async_computation | async-start | bytes 524288 | tf_op jit(solution)/shard_map/all_to_all | solution.py:319
  33.9 14.3 %collective-permute-start.2 = (bf16[8,32,512]{2,1,0:T(8,128)(2,1)S(1)}, bf16[8,32,512]{2,1,0:T(8,128)(2,1)S(1)}, u32[]{:S(2)}, u32[]{:S(2)}) collective-permute-start(bf16[8,32,512]{2,1,0:T(8,128)(2,1)S(1)} %all-to-all-done.x0_ref), channel_id=1, source_target_pairs={{0,1},{1,0},{2,3},{3,2},{4,5},{5,4},{6,7},{7,6},{8,9},{9,8},{10,11... | collective-permute-start | bytes 786440 | tf_op jit(solution)/shard_map/ppermute | solution.py:320
  33.9 14.3 %collective-permute-start.3 = (bf16[8,32,512]{2,1,0:T(8,128)(2,1)S(1)}, bf16[8,32,512]{2,1,0:T(8,128)(2,1)S(1)}, u32[]{:S(2)}, u32[]{:S(2)}) collective-permute-start(bf16[8,32,512]{2,1,0:T(8,128)(2,1)S(1)} %all-to-all-done.x0_ref), channel_id=1, source_target_pairs={{0,2},{1,3},{2,0},{3,1},{4,6},{5,7},{6,4},{7,5},{8,10},{9,11},{10,... | collective-permute-start | bytes 786440 | tf_op jit(solution)/shard_map/ppermute | solution.py:320
  34.5 13.8 %collective-permute-start.4 = (bf16[8,32,512]{2,1,0:T(8,128)(2,1)S(1)}, bf16[8,32,512]{2,1,0:T(8,128)(2,1)S(1)}, u32[]{:S(2)}, u32[]{:S(2)}) collective-permute-start(bf16[8,32,512]{2,1,0:T(8,128)(2,1)S(1)} %all-to-all-done.x0_ref), channel_id=1, source_target_pairs={{0,3},{1,2},{2,1},{3,0},{4,7},{5,6},{6,5},{7,4},{8,11},{9,10},{10,... | collective-permute-start | bytes 786440 | tf_op jit(solution)/shard_map/ppermute | solution.py:320
  35.8 7.2 %collective-permute-start.1 = (s32[2,136,128]{2,1,0:T(8,128)S(1)}, s32[2,136,128]{2,1,0:T(8,128)S(1)}, u32[]{:S(2)}, u32[]{:S(2)}) collective-permute-start(s32[2,136,128]{2,1,0:T(8,128)S(1)} %constant_dynamic-slice_fusion.1), channel_id=1, source_target_pairs={{0,18},{2,16},{16,2},{18,0},{1,19},{3,17},{17,3},{19,1},{4,22},{6,... | collective-permute-start | bytes 417800 | tf_op jit(solution)/shard_map/ppermute | solution.py:313
  48.3 38.4 %all-to-all-start.1 = ((s32[32,136,128]{2,1,0:T(8,128)}), s32[32,136,128]{2,1,0:T(8,128)}, u32[]{:S(2)}, u32[]{:S(2)}) async-start(s32[32,136,128]{2,1,0:T(8,128)} %shard_map.92), calls=%async_computation.1 | async-start | bytes 4456448 | tf_op jit(solution)/shard_map/all_to_all | solution.py:324
  54.7 10.1 %copy-start.12 = (s32[32]{0:T(128)S(1)}, s32[32]{0:T(128)}, u32[]{:S(2)}) copy-start(s32[32]{0:T(128)} %param.13) | copy-start | bytes 388
  54.7 1.6 copy-start.8
  58.9 36.2 %collective-permute-start.5 = (s32[520,128]{1,0:T(8,128)S(1)}, s32[520,128]{1,0:T(8,128)S(1)}, u32[]{:S(2)}, u32[]{:S(2)}) collective-permute-start(s32[520,128]{1,0:T(8,128)S(1)} %get-tuple-element.37), channel_id=1, source_target_pairs={{0,4},{4,8},{8,12},{12,0},{1,5},{5,9},{9,13},{13,1},{2,6},{6,10},{... | collective-permute-start | bytes 798728 | tf_op jit(solution)/shard_map/ppermute | solution.py:347
  60.7 34.4 %collective-permute-start.6 = (s32[520,128]{1,0:T(8,128)S(1)}, s32[520,128]{1,0:T(8,128)S(1)}, u32[]{:S(2)}, u32[]{:S(2)}) collective-permute-start(s32[520,128]{1,0:T(8,128)S(1)} %get-tuple-element.38), channel_id=1, source_target_pairs={{0,8},{4,12},{8,0},{12,4},{1,9},{5,13},{9,1},{13,5},{2,10},{6,14},... | collective-permute-start | bytes 798728 | tf_op jit(solution)/shard_map/ppermute | solution.py:347
  63.3 34.6 %collective-permute-start.7 = (s32[520,128]{1,0:T(8,128)S(1)}, s32[520,128]{1,0:T(8,128)S(1)}, u32[]{:S(2)}, u32[]{:S(2)}) collective-permute-start(s32[520,128]{1,0:T(8,128)S(1)} %get-tuple-element.39), channel_id=1, source_target_pairs={{0,12},{4,0},{8,4},{12,8},{1,13},{5,1},{9,5},{13,9},{2,14},{6,2},{... | collective-permute-start | bytes 798728 | tf_op jit(solution)/shard_map/ppermute | solution.py:347
  99.5 36.2 %all-to-all-start.2 = ((s32[32,136,128]{2,1,0:T(8,128)}), s32[32,136,128]{2,1,0:T(8,128)}, u32[]{:S(2)}, u32[]{:S(2)}) async-start(s32[32,136,128]{2,1,0:T(8,128)} %broadcast_in_dim.8), calls=%async_computation.2 | async-start | bytes 4456448 | tf_op jit(solution)/shard_map/all_to_all | solution.py:334
  105.0 43.9 %all-gather.7.cloned.1.call-start = ((), (), s32[]{:S(2)}) async-start(), calls=%async_computation.6 | async-start | bytes 1392640 | tf_op jit(solution)/shard_map/all_gather | solution.py:329
  141.6 1.4 copy-start.1
  142.9 15.7 %all-to-all-start.3 = ((f32[8,128,128]{2,1,0:T(8,128)}), f32[8,128,128]{2,1,0:T(8,128)S(1)}, u32[]{:S(2)}, u32[]{:S(2)}) async-start(f32[8,128,128]{2,1,0:T(8,128)} %get-tuple-element.45), calls=%async_computation.3 | async-start | bytes 1048576 | tf_op jit(solution)/shard_map/all_to_all | solution.py:337
  148.9 4.3 %copy-start = (s32[8,2,136,128]{3,2,1,0:T(8,128)S(1)}, s32[8,2,136,128]{3,2,1,0:T(8,128)}, u32[]{:S(2)}) copy-start(s32[8,2,136,128]{3,2,1,0:T(8,128)} %all-gather.7.cloned.1.call-done) | copy-start | bytes 3342340
  150.3 1.6 collective-permute-start.11
  150.4 1.9 %collective-permute-start.10 = (s32[2,2,136,128]{3,2,1,0:T(8,128)S(1)}, s32[2,2,136,128]{3,2,1,0:T(8,128)S(1)}, u32[]{:S(2)}, u32[]{:S(2)}) collective-permute-start(s32[2,2,136,128]{3,2,1,0:T(8,128)S(1)} %get-tuple-element.55), channel_id=1, source_target_pairs={{0,1},{1,0},{2,3},{3,2},{4,5},{5,4},{6,7},{7,6},{8,9},{9,8},{10,11... | collective-permute-start | bytes 835592 | tf_op jit(solution)/shard_map/ppermute | solution.py:351
  150.9 1.8 collective-permute-start.9
  151.0 2.1 %collective-permute-start.8 = (s32[2,2,136,128]{3,2,1,0:T(8,128)S(1)}, s32[2,2,136,128]{3,2,1,0:T(8,128)S(1)}, u32[]{:S(2)}, u32[]{:S(2)}) collective-permute-start(s32[2,2,136,128]{3,2,1,0:T(8,128)S(1)} %get-tuple-element.53), channel_id=1, source_target_pairs={{0,1},{1,0},{2,3},{3,2},{4,5},{5,4},{6,7},{7,6},{8,9},{9,8},{10,11... | collective-permute-start | bytes 835592 | tf_op jit(solution)/shard_map/ppermute | solution.py:351
  157.1 1.4 copy-start.9
  158.7 1.6 copy-start.10
  160.2 1.6 copy-start.11
  161.8 20.9 %copy-start.2 = (bf16[1024,1024]{1,0:T(8,128)(2,1)S(1)}, bf16[1024,1024]{1,0:T(8,128)(2,1)}, u32[]{:S(2)}) copy-start(bf16[1024,1024]{1,0:T(8,128)(2,1)} %copy-done.1) | copy-start | bytes 6291460
Sparse Core Ops, SparseCore 0:
  18.1 33.4 all-gather.4
  107.5 37.4 all-gather.6
where the time goes:
time: 193 us; the launch traced here: 192 us
  waiting for transfers between devices  80.1 us (42%)
  starting transfers between devices  37.7 us (20%)
  Pallas kernels  25.4 us (13%)
  blocking collectives  18.7 us (10%)
  local copies, waits for them, and re-layouts  13.8 us (7%)
  between operations  13.7 us (7%)
  other arithmetic  2.6 us (1%)
    all_to_all x1, waiting for transfers between devices, body(): lax.all_to_all(jnp.broadcast_to(piece, spread.shape), ALL_DP, 0, 0, tiled...  30 us
    all_to_all x1, waiting for transfers between devices, body(): spread = lax.all_to_all(packed, ALL_DP, 0, 0, tiled=True)  21.8 us
    all_to_all x1, blocking collectives, body(): u = lax.all_to_all(u, PAIR, 0, 0, tiled=True)  18.7 us
    ppermute x3, waiting for transfers between devices, along(): return lax.ppermute(block, axis, [(i, (i + shift) % 4) for i in range(4)])  10.3 us
    unnamed x26, local copies, waits for them, and re-layouts  9.2 us
    all_to_all x1, waiting for transfers between devices, body(): moved = lax.all_to_all(chunks, ('y', 'h'), 0, 0, tiled=True)  8.41 us
    all_to_all x1, starting transfers between devices, body(): moved = lax.all_to_all(chunks, ('y', 'h'), 0, 0, tiled=True)  7.17 us
    ppermute x1, waiting for transfers between devices, body(): lax.ppermute(in_part, ('h', 'l'), [(i, 3 - i) for i in range(4)])  6.47 us
  transfers between devices with their start and end apart: 18, of which 12 were waited for; matrix products, arithmetic and copies ran while one was open for 2% of the time, Pallas kernels for 11%

commit v1 on v0

--- a/solution.py
+++ b/solution.py
@@ -332,10 +332,11 @@
     piece, words = lax.optimization_barrier((piece, words))
 
     got = lax.all_to_all(jnp.broadcast_to(piece, spread.shape), ALL_DP, 0, 0, tiled=True)
+    in_high, in_low, in_side = unpack_basis(me, in_all, jnp.stack([flip(in_all[z], "c") for z in range(4)]))
+    own, in_high, in_low = lax.optimization_barrier((own, in_high, in_low))
     v, out_high, out_low = front(got, own, words)
 
     v = lax.all_to_all(v, PAIR, 0, 0, tiled=True)
-    in_high, in_low, in_side = unpack_basis(me, in_all, jnp.stack([flip(in_all[z], "c") for z in range(4)]))
     u = middle(v, in_high, in_low, in_side, piece)
     u = lax.all_to_all(u, PAIR, 0, 0, tiled=True)
     return back(u, out_high, out_low)

time: 193 us -> 190 us (0.984)
  blocking collectives: 18.7 us -> 28.7 us
  starting transfers between devices: 37.7 us -> 31.5 us
  local copies, waits for them, and re-layouts: 13.8 us -> 7.82 us
    all_to_all x0 -> x1, blocking collectives: none -> 15.4 us  [body(): v = lax.all_to_all(v, PAIR, 0, 0, tiled=True)]
    ppermute x3, waiting for transfers between devices: 10.3 us -> 19.3 us  [along(): return lax.ppermute(block, axis, [(i, (i + shift) % 4) for i in range(4)])]
    all_to_all x1, waiting for transfers between devices: 30 us -> 22.4 us  [body(): lax.all_to_all(jnp.broadcast_to(piece, spread.shape), ALL_DP, 0, 0, tiled...]
    all_to_all x1 -> x0, starting transfers between devices: 5.93 us -> none  [body(): v = lax.all_to_all(v, PAIR, 0, 0, tiled=True)]
    unnamed x26 -> x18, local copies, waits for them, and re-layouts: 9.2 us -> 3.28 us
    all_to_all x1, blocking collectives: 18.7 us -> 13.2 us  [body(): u = lax.all_to_all(u, PAIR, 0, 0, tiled=True)]
  transfers between devices with their start and end apart: 18 -> 17, of which waited for: 12 -> 12; matrix products, arithmetic and copies ran while one was open for 2% -> 3% of each run, Pallas kernels for 11% -> 8%
where the time goes in v1:
time: 190 us; the launch traced here: 189 us
  waiting for transfers between devices  80.1 us (42%)
  starting transfers between devices  31.5 us (17%)
  blocking collectives  28.7 us (15%)
  Pallas kernels  24.8 us (13%)
  between operations  13.7 us (7%)
  local copies, waits for them, and re-layouts  7.82 us (4%)
  other arithmetic  2.6 us (1%)
    all_to_all x1, waiting for transfers between devices, body(): lax.all_to_all(jnp.broadcast_to(piece, spread.shape), ALL_DP, 0, 0, tiled...  22.4 us
    all_to_all x1, waiting for transfers between devices, body(): spread = lax.all_to_all(packed, ALL_DP, 0, 0, tiled=True)  21.5 us
    ppermute x3, waiting for transfers between devices, along(): return lax.ppermute(block, axis, [(i, (i + shift) % 4) for i in range(4)])  19.3 us
    all_to_all x1, blocking collectives, body(): v = lax.all_to_all(v, PAIR, 0, 0, tiled=True)  15.4 us
    all_to_all x1, blocking collectives, body(): u = lax.all_to_all(u, PAIR, 0, 0, tiled=True)  13.2 us
    all_to_all x1, waiting for transfers between devices, body(): moved = lax.all_to_all(chunks, ('y', 'h'), 0, 0, tiled=True)  8.41 us
    all_to_all x1, starting transfers between devices, body(): moved = lax.all_to_all(chunks, ('y', 'h'), 0, 0, tiled=True)  7.17 us
    all_to_all x1, starting transfers between devices, body(): spread = lax.all_to_all(packed, ALL_DP, 0, 0, tiled=True)  6.35 us
  transfers between devices with their start and end apart: 17, of which 12 were waited for; matrix products, arithmetic and copies ran while one was open for 3% of the time, Pallas kernels for 8%

profile of v1, /device:TPU:0, one launch (start us, length us, event | category | flops | bytes accessed | tf_op | source)
XLA Modules:
  0.0 189.1 jit_solution(1814373892882900111)
XLA Ops:
  6.5 3.1 %collective-permute-start = (bf16[128,1024]{1,0:T(8,128)(2,1)}, bf16[128,1024]{1,0:T(8,128)(2,1)S(1)}, u32[]{:S(2)}, u32[]{:S(2)}) collective-permute-start(bf16[128,1024]{1,0:T(8,128)(2,1)} %bitcast.32), channel_id=1, source_target_pairs={{0,16},{16,0},{1,17},{17,1},{2,18},{18,2},{3,19},{19,3},{4,20},{20... | collective-permute-start | bytes 786440 | tf_op jit(solution)/shard_map/ppermute | solution.py:352
  9.6 0.7 concatenate.3.me_ref
  10.4 0.9 copy-done.2
  11.3 0.7 copy-done.3
  12.1 3.6 %shard_map.91 = bf16[8,32,512]{2,1,0:T(8,128)(2,1)} custom-call(s32[8]{0:T(128)S(1)} %concatenate.3.me_ref, s32[1,4096]{1,0:T(1,128)S(1)} %copy-done.3, bf16[32,4096]{1,0:T(8,128)(2,1)S(1)} %bitcast.24), custom_call_target="tpu_custom_call" | custom-call | flops 1000000 | bytes 1000000 | tf_op jit(solution)/shard_map/pallas_call | solution.py:52
  15.7 0.5 collective-permute-done
  16.2 1.8 pad_maximum_fusion
  18.0 7.2 %all-to-all-start = ((bf16[8,32,512]{2,1,0:T(8,128)(2,1)}), bf16[8,32,512]{2,1,0:T(8,128)(2,1)S(1)}, u32[]{:S(2)}, u32[]{:S(2)}) async-start(bf16[8,32,512]{2,1,0:T(8,128)(2,1)} %shard_map.91), calls=%async_computation | async-start | bytes 524288 | tf_op jit(solution)/shard_map/all_to_all | solution.py:319
  25.2 0.4 shard_map.93
  25.5 8.4 %all-to-all-done.x0_ref = bf16[8,32,512]{2,1,0:T(8,128)(2,1)S(1)} async-done(((bf16[8,32,512]{2,1,0:T(8,128)(2,1)}), bf16[8,32,512]{2,1,0:T(8,128)(2,1)S(1)}, u32[]{:S(2)}, u32[]{:S(2)}) %all-to-all-start) | async-done | bytes 262176 | tf_op jit(solution)/shard_map/all_to_all | solution.py:319
  33.9 0.6 collective-permute-start.3
  34.6 1.2 collective-permute-start.2
  35.8 0.7 collective-permute-start.1
  36.5 6.2 %collective-permute-done.1 = s32[2,136,128]{2,1,0:T(8,128)S(1)} collective-permute-done((s32[2,136,128]{2,1,0:T(8,128)S(1)}, s32[2,136,128]{2,1,0:T(8,128)S(1)}, u32[]{:S(2)}, u32[]{:S(2)}) %collective-permute-start.1) | collective-permute-done | bytes 139296 | tf_op jit(solution)/shard_map/ppermute | solution.py:313
  42.7 0.7 pad_add_fusion.1
  43.4 4.6 %shard_map.92 = s32[32,136,128]{2,1,0:T(8,128)} custom-call(f32[1024,1024]{1,0:T(8,128)} %bitcast.27, f32[1,1024]{1,0:T(1,128)S(1)} %copy-done.4), custom_call_target="tpu_custom_call" | custom-call | flops 10240000 | bytes 6144000 | tf_op jit(solution)/shard_map/pallas_call | solution.py:113
  48.0 6.4 %all-to-all-start.1 = ((s32[32,136,128]{2,1,0:T(8,128)}), s32[32,136,128]{2,1,0:T(8,128)}, u32[]{:S(2)}, u32[]{:S(2)}) async-start(s32[32,136,128]{2,1,0:T(8,128)} %shard_map.92), calls=%async_computation.1 | async-start | bytes 4456448 | tf_op jit(solution)/shard_map/all_to_all | solution.py:324
  54.4 0.0 all-gather.7.cloned.1.call-start
  54.5 1.6 copy-done.6
  56.1 2.6 %shard_map.94 = (f32[128,1024]{1,0:T(8,128)S(1)}, s32[520,128]{1,0:T(8,128)S(1)}, s32[520,128]{1,0:T(8,128)S(1)}, s32[520,128]{1,0:T(8,128)S(1)}) custom-call(s32[8]{0:T(128)S(1)} %concatenate.3.me_ref, bf16[8,32,512]{2,1,0:T(8,128)(2,1)S(1)} %all-to-all-done.x0_ref, bf16[8,32,512]{2,1,0:T(8,128)(2,1)S(1)} %collective-permute-done.2.x1_ref, ...), custom_call_target="tpu_custom_call" | custom-call | flops 1000000000 | bytes 5000000 | tf_op jit(solution)/shard_map/pallas_call | solution.py:190
  58.6 1.8 collective-permute-start.5
  60.4 2.7 %collective-permute-start.6 = (s32[520,128]{1,0:T(8,128)S(1)}, s32[520,128]{1,0:T(8,128)S(1)}, u32[]{:S(2)}, u32[]{:S(2)}) collective-permute-start(s32[520,128]{1,0:T(8,128)S(1)} %get-tuple-element.41), channel_id=1, source_target_pairs={{0,8},{4,12},{8,0},{12,4},{1,9},{5,13},{9,1},{13,5},{2,10},{6,14},... | collective-permute-start | bytes 798728 | tf_op jit(solution)/shard_map/ppermute | solution.py:348
  63.1 1.5 collective-permute-start.7
  64.7 21.5 %all-to-all-done.1 = s32[32,136,128]{2,1,0:T(8,128)} async-done(((s32[32,136,128]{2,1,0:T(8,128)}), s32[32,136,128]{2,1,0:T(8,128)}, u32[]{:S(2)}, u32[]{:S(2)}) %all-to-all-start.1) | async-done | bytes 2228256 | tf_op jit(solution)/shard_map/all_to_all | solution.py:324
  86.2 0.9 constant_dynamic-slice_fusion.out_side_ref
  87.1 10.2 %collective-permute-done.5.w1_ref = s32[520,128]{1,0:T(8,128)S(1)} collective-permute-done((s32[520,128]{1,0:T(8,128)S(1)}, s32[520,128]{1,0:T(8,128)S(1)}, u32[]{:S(2)}, u32[]{:S(2)}) %collective-permute-start.5) | collective-permute-done | bytes 266272 | tf_op jit(solution)/shard_map/ppermute | solution.py:348
  97.3 5.1 %collective-permute-done.6.w2_ref = s32[520,128]{1,0:T(8,128)S(1)} collective-permute-done((s32[520,128]{1,0:T(8,128)S(1)}, s32[520,128]{1,0:T(8,128)S(1)}, u32[]{:S(2)}, u32[]{:S(2)}) %collective-permute-start.6) | collective-permute-done | bytes 266272 | tf_op jit(solution)/shard_map/ppermute | solution.py:348
  102.4 4.0 %collective-permute-done.7.w3_ref = s32[520,128]{1,0:T(8,128)S(1)} collective-permute-done((s32[520,128]{1,0:T(8,128)S(1)}, s32[520,128]{1,0:T(8,128)S(1)}, u32[]{:S(2)}, u32[]{:S(2)}) %collective-permute-start.7) | collective-permute-done | bytes 266272 | tf_op jit(solution)/shard_map/ppermute | solution.py:348
  106.4 1.5 broadcast_in_dim.8
  107.9 5.2 %all-to-all-start.2 = ((s32[32,136,128]{2,1,0:T(8,128)}), s32[32,136,128]{2,1,0:T(8,128)}, u32[]{:S(2)}, u32[]{:S(2)}) async-start(s32[32,136,128]{2,1,0:T(8,128)} %broadcast_in_dim.8), calls=%async_computation.2 | async-start | bytes 4456448 | tf_op jit(solution)/shard_map/all_to_all | solution.py:334
  113.1 0.0 all-gather.7.cloned.1.call-done
  113.2 1.4 fusion
  114.6 0.1 collective-permute-start.8
  114.7 0.5 collective-permute-start.11
  115.2 0.1 collective-permute-start.10
  115.3 0.4 collective-permute-start.9
  115.7 0.5 collective-permute-done.8
  116.2 0.4 collective-permute-done.11
  116.6 0.4 collective-permute-done.10
  117.0 0.4 collective-permute-done.9
  117.4 0.1 pad_add_fusion.other_ref
  117.5 3.9 %shard_map.95 = (bf16[1024,1024]{1,0:T(8,128)(2,1)S(1)}, bf16[1024,1024]{1,0:T(8,128)(2,1)}, s32[8,8,128]{2,1,0:T(8,128)S(1)}) custom-call(s32[8]{0:T(128)S(1)} %concatenate.3.me_ref, s32[4,2,2,136,128]{4,3,2,1,0:T(8,128)S(1)} %bitcast.22, s32[4,2,2,136,128]{4,3,2,1,0:T(8,128)S(1)} %pad_add_fusion.other_ref), custom_call_target="tpu_custom_call" | custom-call | flops 10000000 | bytes 6000000 | tf_op jit(solution)/shard_map/pallas_call | solution.py:150
  121.4 22.4 %all-to-all-done.2.got_ref = s32[32,136,128]{2,1,0:T(8,128)} async-done(((s32[32,136,128]{2,1,0:T(8,128)}), s32[32,136,128]{2,1,0:T(8,128)}, u32[]{:S(2)}, u32[]{:S(2)}) %all-to-all-start.2) | async-done | bytes 2228256 | tf_op jit(solution)/shard_map/all_to_all | solution.py:334
  143.8 5.2 %shard_map.96 = (f32[8,128,128]{2,1,0:T(8,128)S(1)}, bf16[1024,1024]{1,0:T(8,128)(2,1)S(1)}, bf16[1024,1024]{1,0:T(8,128)(2,1)S(1)}) custom-call(s32[32,136,128]{2,1,0:T(8,128)} %all-to-all-done.2.got_ref, f32[128,1024]{1,0:T(8,128)S(1)} %get-tuple-element.49.own_ref, s32[520,128]{1,0:T(8,128)S(1)} %collective-permute-done.5.w1_ref, ...), custom_call_target="tpu_custom_call" | custom-call | flops 800000000 | bytes 8000000 | tf_op jit(solution)/shard_map/pallas_call | solution.py:226
  149.1 15.4 %all_to_all.25.v_ref = f32[8,128,128]{2,1,0:T(8,128)S(1)} all-to-all(f32[8,128,128]{2,1,0:T(8,128)S(1)} %get-tuple-element.53), channel_id=1, replica_groups=mesh['y'=4,'h'=2,'z'=4,'l'=2,'c'=2] {'h','z'}, dimensions={0} | all-to-all | bytes 1048576 | tf_op jit(solution)/shard_map/all_to_all | solution.py:339
  164.5 2.3 %shard_map.97 = f32[8,128,128]{2,1,0:T(8,128)S(1)} custom-call(f32[8,128,128]{2,1,0:T(8,128)S(1)} %all_to_all.25.v_ref, bf16[1024,1024]{1,0:T(8,128)(2,1)S(1)} %get-tuple-element.54.high_ref, bf16[1024,1024]{1,0:T(8,128)(2,1)S(1)} %copy-done.7, s32[8,8,128]{2,1,0:T(8,128)S(1)} %get-tuple-element.56.in_side_ref, ...), custom_call_target="tpu_custom_call" | custom-call | flops 1600000000 | bytes 6000000 | tf_op jit(solution)/shard_map/pallas_call | solution.py:258
  166.8 13.2 %all_to_all.26.u_ref = f32[8,128,128]{2,1,0:T(8,128)S(1)} all-to-all(f32[8,128,128]{2,1,0:T(8,128)S(1)} %shard_map.97), channel_id=1, replica_groups=mesh['y'=4,'h'=2,'z'=4,'l'=2,'c'=2] {'h','z'}, dimensions={0} | all-to-all | bytes 1048576 | tf_op jit(solution)/shard_map/all_to_all | solution.py:341
  180.0 2.3 %shard_map.98 = f32[128,1024]{1,0:T(8,128)} custom-call(f32[8,128,128]{2,1,0:T(8,128)S(1)} %all_to_all.26.u_ref, bf16[1024,1024]{1,0:T(8,128)(2,1)S(1)} %get-tuple-element.57.high_ref, bf16[1024,1024]{1,0:T(8,128)(2,1)S(1)} %get-tuple-element.58.low_ref), custom_call_target="tpu_custom_call" | custom-call | flops 800000000 | bytes 5000000 | tf_op jit(solution)/shard_map/pallas_call | solution.py:282
  (25 shorter events, 0.1 us)
Async XLA Ops:
  6.5 18.6 %copy-start.1 = (f32[128,1024]{1,0:T(8,128)S(1)}, f32[128,1024]{1,0:T(8,128)}, u32[]{:S(2)}) copy-start(f32[128,1024]{1,0:T(8,128)} %basis_ref.1) | copy-start | bytes 1572868
  6.5 47.9 %all-gather.5.cloned.1.call-start = ((), (), s32[]{:S(2)}) async-start(), calls=%async_computation.5 | async-start | bytes 2621440 | tf_op jit(solution)/shard_map/all_gather | solution.py:327
  6.5 9.6 %collective-permute-start = (bf16[128,1024]{1,0:T(8,128)(2,1)}, bf16[128,1024]{1,0:T(8,128)(2,1)S(1)}, u32[]{:S(2)}, u32[]{:S(2)}) collective-permute-start(bf16[128,1024]{1,0:T(8,128)(2,1)} %bitcast.32), channel_id=1, source_target_pairs={{0,16},{16,0},{1,17},{17,1},{2,18},{18,2},{3,19},{19,3},{4,20},{20... | collective-permute-start | bytes 786440 | tf_op jit(solution)/shard_map/ppermute | solution.py:352
  10.4 1.0 copy-start.2
  11.3 0.7 copy-start.3
  12.0 13.1 %copy-start.5 = (f32[128]{0:T(128)S(1)}, f32[128]{0:T(128)}, u32[]{:S(2)}) copy-start(f32[128]{0:T(128)} %param.15) | copy-start | bytes 1540
  15.7 27.7 %copy-start.4 = (f32[1,1024]{1,0:T(1,128)S(1)}, f32[1,1024]{1,0:T(1,128)}, u32[]{:S(2)}) copy-start(f32[1,1024]{1,0:T(1,128)} %values_ref.1) | copy-start | bytes 12292
  18.0 16.0 %all-to-all-start = ((bf16[8,32,512]{2,1,0:T(8,128)(2,1)}), bf16[8,32,512]{2,1,0:T(8,128)(2,1)S(1)}, u32[]{:S(2)}, u32[]{:S(2)}) async-start(bf16[8,32,512]{2,1,0:T(8,128)(2,1)} %shard_map.91), calls=%async_computation | async-start | bytes 524288 | tf_op jit(solution)/shard_map/all_to_all | solution.py:319
  33.9 14.1 %collective-permute-start.4 = (bf16[8,32,512]{2,1,0:T(8,128)(2,1)S(1)}, bf16[8,32,512]{2,1,0:T(8,128)(2,1)S(1)}, u32[]{:S(2)}, u32[]{:S(2)}) collective-permute-start(bf16[8,32,512]{2,1,0:T(8,128)(2,1)S(1)} %all-to-all-done.x0_ref), channel_id=1, source_target_pairs={{0,3},{1,2},{2,1},{3,0},{4,7},{5,6},{6,5},{7,4},{8,11},{9,10},{10,... | collective-permute-start | bytes 786440 | tf_op jit(solution)/shard_map/ppermute | solution.py:320
  33.9 14.1 %collective-permute-start.3 = (bf16[8,32,512]{2,1,0:T(8,128)(2,1)S(1)}, bf16[8,32,512]{2,1,0:T(8,128)(2,1)S(1)}, u32[]{:S(2)}, u32[]{:S(2)}) collective-permute-start(bf16[8,32,512]{2,1,0:T(8,128)(2,1)S(1)} %all-to-all-done.x0_ref), channel_id=1, source_target_pairs={{0,2},{1,3},{2,0},{3,1},{4,6},{5,7},{6,4},{7,5},{8,10},{9,11},{10,... | collective-permute-start | bytes 786440 | tf_op jit(solution)/shard_map/ppermute | solution.py:320
  34.6 13.5 %collective-permute-start.2 = (bf16[8,32,512]{2,1,0:T(8,128)(2,1)S(1)}, bf16[8,32,512]{2,1,0:T(8,128)(2,1)S(1)}, u32[]{:S(2)}, u32[]{:S(2)}) collective-permute-start(bf16[8,32,512]{2,1,0:T(8,128)(2,1)S(1)} %all-to-all-done.x0_ref), channel_id=1, source_target_pairs={{0,1},{1,0},{2,3},{3,2},{4,5},{5,4},{6,7},{7,6},{8,9},{9,8},{10,11... | collective-permute-start | bytes 786440 | tf_op jit(solution)/shard_map/ppermute | solution.py:320
  35.8 6.9 %collective-permute-start.1 = (s32[2,136,128]{2,1,0:T(8,128)S(1)}, s32[2,136,128]{2,1,0:T(8,128)S(1)}, u32[]{:S(2)}, u32[]{:S(2)}) collective-permute-start(s32[2,136,128]{2,1,0:T(8,128)S(1)} %constant_dynamic-slice_fusion.1), channel_id=1, source_target_pairs={{0,18},{2,16},{16,2},{18,0},{1,19},{3,17},{17,3},{19,1},{4,22},{6,... | collective-permute-start | bytes 417800 | tf_op jit(solution)/shard_map/ppermute | solution.py:313
  48.0 38.2 %all-to-all-start.1 = ((s32[32,136,128]{2,1,0:T(8,128)}), s32[32,136,128]{2,1,0:T(8,128)}, u32[]{:S(2)}, u32[]{:S(2)}) async-start(s32[32,136,128]{2,1,0:T(8,128)} %shard_map.92), calls=%async_computation.1 | async-start | bytes 4456448 | tf_op jit(solution)/shard_map/all_to_all | solution.py:324
  54.4 10.2 %copy-start.8 = (s32[32]{0:T(128)S(1)}, s32[32]{0:T(128)}, u32[]{:S(2)}) copy-start(s32[32]{0:T(128)} %param.13) | copy-start | bytes 388
  54.4 58.8 %all-gather.7.cloned.1.call-start = ((), (), s32[]{:S(2)}) async-start(), calls=%async_computation.6 | async-start | bytes 1392640 | tf_op jit(solution)/shard_map/all_gather | solution.py:329
  54.5 1.6 copy-start.6
  58.6 38.7 %collective-permute-start.5 = (s32[520,128]{1,0:T(8,128)S(1)}, s32[520,128]{1,0:T(8,128)S(1)}, u32[]{:S(2)}, u32[]{:S(2)}) collective-permute-start(s32[520,128]{1,0:T(8,128)S(1)} %get-tuple-element.40), channel_id=1, source_target_pairs={{0,4},{4,8},{8,12},{12,0},{1,5},{5,9},{9,13},{13,1},{2,6},{6,10},{... | collective-permute-start | bytes 798728 | tf_op jit(solution)/shard_map/ppermute | solution.py:348
  60.4 42.0 %collective-permute-start.6 = (s32[520,128]{1,0:T(8,128)S(1)}, s32[520,128]{1,0:T(8,128)S(1)}, u32[]{:S(2)}, u32[]{:S(2)}) collective-permute-start(s32[520,128]{1,0:T(8,128)S(1)} %get-tuple-element.41), channel_id=1, source_target_pairs={{0,8},{4,12},{8,0},{12,4},{1,9},{5,13},{9,1},{13,5},{2,10},{6,14},... | collective-permute-start | bytes 798728 | tf_op jit(solution)/shard_map/ppermute | solution.py:348
  63.1 43.3 %collective-permute-start.7 = (s32[520,128]{1,0:T(8,128)S(1)}, s32[520,128]{1,0:T(8,128)S(1)}, u32[]{:S(2)}, u32[]{:S(2)}) collective-permute-start(s32[520,128]{1,0:T(8,128)S(1)} %get-tuple-element.42), channel_id=1, source_target_pairs={{0,12},{4,0},{8,4},{12,8},{1,13},{5,1},{9,5},{13,9},{2,14},{6,2},{... | collective-permute-start | bytes 798728 | tf_op jit(solution)/shard_map/ppermute | solution.py:348
  107.9 35.9 %all-to-all-start.2 = ((s32[32,136,128]{2,1,0:T(8,128)}), s32[32,136,128]{2,1,0:T(8,128)}, u32[]{:S(2)}, u32[]{:S(2)}) async-start(s32[32,136,128]{2,1,0:T(8,128)} %broadcast_in_dim.8), calls=%async_computation.2 | async-start | bytes 4456448 | tf_op jit(solution)/shard_map/all_to_all | solution.py:334
  113.2 4.3 %copy-start = (s32[8,2,136,128]{3,2,1,0:T(8,128)S(1)}, s32[8,2,136,128]{3,2,1,0:T(8,128)}, u32[]{:S(2)}) copy-start(s32[8,2,136,128]{3,2,1,0:T(8,128)} %all-gather.7.cloned.1.call-done) | copy-start | bytes 3342340
  114.6 1.6 collective-permute-start.8
  114.7 1.9 %collective-permute-start.11 = (s32[2,2,136,128]{3,2,1,0:T(8,128)S(1)}, s32[2,2,136,128]{3,2,1,0:T(8,128)S(1)}, u32[]{:S(2)}, u32[]{:S(2)}) collective-permute-start(s32[2,2,136,128]{3,2,1,0:T(8,128)S(1)} %get-tuple-element.60), channel_id=1, source_target_pairs={{0,1},{1,0},{2,3},{3,2},{4,5},{5,4},{6,7},{7,6},{8,9},{9,8},{10,11... | collective-permute-start | bytes 835592 | tf_op jit(solution)/shard_map/ppermute | solution.py:352
  115.2 1.8 collective-permute-start.10
  115.3 2.1 %collective-permute-start.9 = (s32[2,2,136,128]{3,2,1,0:T(8,128)S(1)}, s32[2,2,136,128]{3,2,1,0:T(8,128)S(1)}, u32[]{:S(2)}, u32[]{:S(2)}) collective-permute-start(s32[2,2,136,128]{3,2,1,0:T(8,128)S(1)} %get-tuple-element.62), channel_id=1, source_target_pairs={{0,1},{1,0},{2,3},{3,2},{4,5},{5,4},{6,7},{7,6},{8,9},{9,8},{10,11... | collective-permute-start | bytes 835592 | tf_op jit(solution)/shard_map/ppermute | solution.py:352
  143.8 20.7 %copy-start.7 = (bf16[1024,1024]{1,0:T(8,128)(2,1)S(1)}, bf16[1024,1024]{1,0:T(8,128)(2,1)}, u32[]{:S(2)}) copy-start(bf16[1024,1024]{1,0:T(8,128)(2,1)} %get-tuple-element.55.low_ref) | copy-start | bytes 6291460
Sparse Core Ops, SparseCore 0:
  18.1 33.4 all-gather.4
  64.7 40.2 all-gather.6

commit v2 on v1

--- a/solution.py
+++ b/solution.py
@@ -325,11 +325,10 @@
     piece = lax.dynamic_index_in_dim(spread, layer_owner[0], 0, keepdims=True)
 
     grads = lax.all_gather(grads, "y")
-    _, in_pair = lax.optimization_barrier((grads, in_pair))
-    in_all = lax.all_gather(in_pair, "z")
     own, *words = partial_rows(me, tokens, grads)
     words = [along(w, "z", k + 1) for k, w in enumerate(words)]
-    piece, words = lax.optimization_barrier((piece, words))
+    piece, in_pair, words = lax.optimization_barrier((piece, in_pair, words))
+    in_all = lax.all_gather(in_pair, "z")
 
     got = lax.all_to_all(jnp.broadcast_to(piece, spread.shape), ALL_DP, 0, 0, tiled=True)
     in_high, in_low, in_side = unpack_basis(me, in_all, jnp.stack([flip(in_all[z], "c") for z in range(4)]))

time: 190 us -> 199 us (1.047)
  waiting for transfers between devices: 80.1 us -> 87.7 us
    all_gather x1, waiting for transfers between devices: 0.02 us -> 38.9 us  [body(): in_all = lax.all_gather(in_pair, 'z')]
    all_to_all x1, waiting for transfers between devices: 22.4 us -> 0.01 us  [body(): lax.all_to_all(jnp.broadcast_to(piece, spread.shape), ALL_DP, 0, 0, tiled...]
    ppermute x3, waiting for transfers between devices: 19.3 us -> 10.4 us  [along(): return lax.ppermute(block, axis, [(i, (i + shift) % 4) for i in range(4)])]
  transfers between devices with their start and end apart: 17 -> 17, of which waited for: 12 -> 11; matrix products, arithmetic and copies ran while one was open for 3% -> 3% of each run, Pallas kernels for 8% -> 8%
where the time goes in v2:
time: 199 us; the launch traced here: 198 us
  waiting for transfers between devices  87.7 us (44%)
  starting transfers between devices  31.6 us (16%)
  blocking collectives  30.3 us (15%)
  Pallas kernels  24.8 us (12%)
  between operations  13.6 us (7%)
  local copies, waits for them, and re-layouts  7.82 us (4%)
  other arithmetic  2.6 us (1%)
    all_gather x1, waiting for transfers between devices, body(): in_all = lax.all_gather(in_pair, 'z')  38.9 us
    all_to_all x1, waiting for transfers between devices, body(): spread = lax.all_to_all(packed, ALL_DP, 0, 0, tiled=True)  21.5 us
    all_to_all x1, blocking collectives, body(): v = lax.all_to_all(v, PAIR, 0, 0, tiled=True)  16.6 us
    all_to_all x1, blocking collectives, body(): u = lax.all_to_all(u, PAIR, 0, 0, tiled=True)  13.7 us
    ppermute x3, waiting for transfers between devices, along(): return lax.ppermute(block, axis, [(i, (i + shift) % 4) for i in range(4)])  10.4 us
    all_to_all x1, waiting for transfers between devices, body(): moved = lax.all_to_all(chunks, ('y', 'h'), 0, 0, tiled=True)  8.41 us
    all_to_all x1, starting transfers between devices, body(): moved = lax.all_to_all(chunks, ('y', 'h'), 0, 0, tiled=True)  7.17 us
    all_to_all x1, starting transfers between devices, body(): spread = lax.all_to_all(packed, ALL_DP, 0, 0, tiled=True)  6.35 us
  transfers between devices with their start and end apart: 17, of which 11 were waited for; matrix products, arithmetic and copies ran while one was open for 3% of the time, Pallas kernels for 8%

profile of v2, /device:TPU:0, one launch (start us, length us, event | category | flops | bytes accessed | tf_op | source)
XLA Modules:
  0.0 198.4 jit_solution(1802449918398906352)
XLA Ops:
  6.5 3.1 %collective-permute-start = (bf16[128,1024]{1,0:T(8,128)(2,1)}, bf16[128,1024]{1,0:T(8,128)(2,1)S(1)}, u32[]{:S(2)}, u32[]{:S(2)}) collective-permute-start(bf16[128,1024]{1,0:T(8,128)(2,1)} %bitcast.32), channel_id=1, source_target_pairs={{0,16},{16,0},{1,17},{17,1},{2,18},{18,2},{3,19},{19,3},{4,20},{20... | collective-permute-start | bytes 786440 | tf_op jit(solution)/shard_map/ppermute | solution.py:351
  9.6 0.7 concatenate.3.me_ref
  10.4 0.9 copy-done.2
  11.3 0.7 copy-done.3
  12.1 3.6 %shard_map.91 = bf16[8,32,512]{2,1,0:T(8,128)(2,1)} custom-call(s32[8]{0:T(128)S(1)} %concatenate.3.me_ref, s32[1,4096]{1,0:T(1,128)S(1)} %copy-done.3, bf16[32,4096]{1,0:T(8,128)(2,1)S(1)} %bitcast.24), custom_call_target="tpu_custom_call" | custom-call | flops 1000000 | bytes 1000000 | tf_op jit(solution)/shard_map/pallas_call | solution.py:52
  15.7 0.5 collective-permute-done
  16.2 1.8 pad_maximum_fusion
  18.0 7.2 %all-to-all-start = ((bf16[8,32,512]{2,1,0:T(8,128)(2,1)}), bf16[8,32,512]{2,1,0:T(8,128)(2,1)S(1)}, u32[]{:S(2)}, u32[]{:S(2)}) async-start(bf16[8,32,512]{2,1,0:T(8,128)(2,1)} %shard_map.91), calls=%async_computation | async-start | bytes 524288 | tf_op jit(solution)/shard_map/all_to_all | solution.py:319
  25.2 0.4 shard_map.93
  25.5 8.4 %all-to-all-done.x0_ref = bf16[8,32,512]{2,1,0:T(8,128)(2,1)S(1)} async-done(((bf16[8,32,512]{2,1,0:T(8,128)(2,1)}), bf16[8,32,512]{2,1,0:T(8,128)(2,1)S(1)}, u32[]{:S(2)}, u32[]{:S(2)}) %all-to-all-start) | async-done | bytes 262176 | tf_op jit(solution)/shard_map/all_to_all | solution.py:319
  33.9 0.6 collective-permute-start.3
  34.6 1.2 collective-permute-start.2
  35.8 0.7 collective-permute-start.1
  36.5 6.2 %collective-permute-done.1 = s32[2,136,128]{2,1,0:T(8,128)S(1)} collective-permute-done((s32[2,136,128]{2,1,0:T(8,128)S(1)}, s32[2,136,128]{2,1,0:T(8,128)S(1)}, u32[]{:S(2)}, u32[]{:S(2)}) %collective-permute-start.1) | collective-permute-done | bytes 139296 | tf_op jit(solution)/shard_map/ppermute | solution.py:313
  42.7 0.7 pad_add_fusion.1
  43.4 4.6 %shard_map.92 = s32[32,136,128]{2,1,0:T(8,128)} custom-call(f32[1024,1024]{1,0:T(8,128)} %bitcast.27, f32[1,1024]{1,0:T(1,128)S(1)} %copy-done.4), custom_call_target="tpu_custom_call" | custom-call | flops 10240000 | bytes 6144000 | tf_op jit(solution)/shard_map/pallas_call | solution.py:113
  48.0 6.4 %all-to-all-start.1 = ((s32[32,136,128]{2,1,0:T(8,128)}), s32[32,136,128]{2,1,0:T(8,128)}, u32[]{:S(2)}, u32[]{:S(2)}) async-start(s32[32,136,128]{2,1,0:T(8,128)} %shard_map.92), calls=%async_computation.1 | async-start | bytes 4456448 | tf_op jit(solution)/shard_map/all_to_all | solution.py:324
  54.4 0.0 all-gather.7.cloned.1.call-start
  54.4 0.0 all-gather.5.cloned.1.call-done
  54.5 1.6 copy-done.6
  56.1 2.6 %shard_map.94 = (f32[128,1024]{1,0:T(8,128)S(1)}, s32[520,128]{1,0:T(8,128)S(1)}, s32[520,128]{1,0:T(8,128)S(1)}, s32[520,128]{1,0:T(8,128)S(1)}) custom-call(s32[8]{0:T(128)S(1)} %concatenate.3.me_ref, bf16[8,32,512]{2,1,0:T(8,128)(2,1)S(1)} %all-to-all-done.x0_ref, bf16[8,32,512]{2,1,0:T(8,128)(2,1)S(1)} %collective-permute-done.2.x1_ref, ...), custom_call_target="tpu_custom_call" | custom-call | flops 1000000000 | bytes 5000000 | tf_op jit(solution)/shard_map/pallas_call | solution.py:190
  58.6 1.8 collective-permute-start.5
  60.4 2.7 %collective-permute-start.6 = (s32[520,128]{1,0:T(8,128)S(1)}, s32[520,128]{1,0:T(8,128)S(1)}, u32[]{:S(2)}, u32[]{:S(2)}) collective-permute-start(s32[520,128]{1,0:T(8,128)S(1)} %get-tuple-element.42), channel_id=1, source_target_pairs={{0,8},{4,12},{8,0},{12,4},{1,9},{5,13},{9,1},{13,5},{2,10},{6,14},... | collective-permute-start | bytes 798728 | tf_op jit(solution)/shard_map/ppermute | solution.py:347
  63.1 1.5 collective-permute-start.7
  64.7 21.5 %all-to-all-done.1 = s32[32,136,128]{2,1,0:T(8,128)} async-done(((s32[32,136,128]{2,1,0:T(8,128)}), s32[32,136,128]{2,1,0:T(8,128)}, u32[]{:S(2)}, u32[]{:S(2)}) %all-to-all-start.1) | async-done | bytes 2228256 | tf_op jit(solution)/shard_map/all_to_all | solution.py:324
  86.2 0.9 constant_dynamic-slice_fusion.out_side_ref
  87.1 7.6 %collective-permute-done.5.w1_ref = s32[520,128]{1,0:T(8,128)S(1)} collective-permute-done((s32[520,128]{1,0:T(8,128)S(1)}, s32[520,128]{1,0:T(8,128)S(1)}, u32[]{:S(2)}, u32[]{:S(2)}) %collective-permute-start.5) | collective-permute-done | bytes 266272 | tf_op jit(solution)/shard_map/ppermute | solution.py:347
  94.7 2.8 %collective-permute-done.7.w3_ref = s32[520,128]{1,0:T(8,128)S(1)} collective-permute-done((s32[520,128]{1,0:T(8,128)S(1)}, s32[520,128]{1,0:T(8,128)S(1)}, u32[]{:S(2)}, u32[]{:S(2)}) %collective-permute-start.7) | collective-permute-done | bytes 266272 | tf_op jit(solution)/shard_map/ppermute | solution.py:347
  97.5 0.0 all-gather.7.cloned.1.call-update
  97.5 1.5 broadcast_in_dim.8
  99.0 5.4 %all-to-all-start.2 = ((s32[32,136,128]{2,1,0:T(8,128)}), s32[32,136,128]{2,1,0:T(8,128)}, u32[]{:S(2)}, u32[]{:S(2)}) async-start(s32[32,136,128]{2,1,0:T(8,128)} %broadcast_in_dim.8), calls=%async_computation.2 | async-start | bytes 4456448 | tf_op jit(solution)/shard_map/all_to_all | solution.py:333
  104.4 38.9 %all-gather.7.cloned.1.call-done = s32[8,2,136,128]{3,2,1,0:T(8,128)} async-done(((s32[2,2,136,128]{3,2,1,0:T(8,128)}), s32[8,2,136,128]{3,2,1,0:T(8,128)}) %all-gather.7.cloned.1.call-update) | async-done | bytes 1114128 | tf_op jit(solution)/shard_map/all_gather | solution.py:331
  143.3 1.4 fusion
  144.7 0.1 collective-permute-start.8
  144.8 0.5 collective-permute-start.11
  145.3 0.1 collective-permute-start.10
  145.4 0.4 collective-permute-start.9
  145.8 0.5 collective-permute-done.8
  146.4 0.4 collective-permute-done.11
  146.8 0.4 collective-permute-done.10
  147.2 0.4 collective-permute-done.9
  147.6 0.1 pad_add_fusion.other_ref
  147.6 3.9 %shard_map.95 = (bf16[1024,1024]{1,0:T(8,128)(2,1)S(1)}, bf16[1024,1024]{1,0:T(8,128)(2,1)}, s32[8,8,128]{2,1,0:T(8,128)S(1)}) custom-call(s32[8]{0:T(128)S(1)} %concatenate.3.me_ref, s32[4,2,2,136,128]{4,3,2,1,0:T(8,128)S(1)} %bitcast.22, s32[4,2,2,136,128]{4,3,2,1,0:T(8,128)S(1)} %pad_add_fusion.other_ref), custom_call_target="tpu_custom_call" | custom-call | flops 10000000 | bytes 6000000 | tf_op jit(solution)/shard_map/pallas_call | solution.py:150
  151.5 5.2 %shard_map.96 = (f32[8,128,128]{2,1,0:T(8,128)S(1)}, bf16[1024,1024]{1,0:T(8,128)(2,1)S(1)}, bf16[1024,1024]{1,0:T(8,128)(2,1)S(1)}) custom-call(s32[32,136,128]{2,1,0:T(8,128)} %all-to-all-done.2.got_ref, f32[128,1024]{1,0:T(8,128)S(1)} %get-tuple-element.49.own_ref, s32[520,128]{1,0:T(8,128)S(1)} %collective-permute-done.5.w1_ref, ...), custom_call_target="tpu_custom_call" | custom-call | flops 800000000 | bytes 8000000 | tf_op jit(solution)/shard_map/pallas_call | solution.py:226
  156.8 16.6 %all_to_all.25.v_ref = f32[8,128,128]{2,1,0:T(8,128)S(1)} all-to-all(f32[8,128,128]{2,1,0:T(8,128)S(1)} %get-tuple-element.53), channel_id=1, replica_groups=mesh['y'=4,'h'=2,'z'=4,'l'=2,'c'=2] {'h','z'}, dimensions={0} | all-to-all | bytes 1048576 | tf_op jit(solution)/shard_map/all_to_all | solution.py:338
  173.4 2.3 %shard_map.97 = f32[8,128,128]{2,1,0:T(8,128)S(1)} custom-call(f32[8,128,128]{2,1,0:T(8,128)S(1)} %all_to_all.25.v_ref, bf16[1024,1024]{1,0:T(8,128)(2,1)S(1)} %get-tuple-element.54.high_ref, bf16[1024,1024]{1,0:T(8,128)(2,1)S(1)} %copy-done.7, s32[8,8,128]{2,1,0:T(8,128)S(1)} %get-tuple-element.56.in_side_ref, ...), custom_call_target="tpu_custom_call" | custom-call | flops 1600000000 | bytes 6000000 | tf_op jit(solution)/shard_map/pallas_call | solution.py:258
  175.6 13.7 %all_to_all.26.u_ref = f32[8,128,128]{2,1,0:T(8,128)S(1)} all-to-all(f32[8,128,128]{2,1,0:T(8,128)S(1)} %shard_map.97), channel_id=1, replica_groups=mesh['y'=4,'h'=2,'z'=4,'l'=2,'c'=2] {'h','z'}, dimensions={0} | all-to-all | bytes 1048576 | tf_op jit(solution)/shard_map/all_to_all | solution.py:340
  189.3 2.3 %shard_map.98 = f32[128,1024]{1,0:T(8,128)} custom-call(f32[8,128,128]{2,1,0:T(8,128)S(1)} %all_to_all.26.u_ref, bf16[1024,1024]{1,0:T(8,128)(2,1)S(1)} %get-tuple-element.57.high_ref, bf16[1024,1024]{1,0:T(8,128)(2,1)S(1)} %get-tuple-element.58.low_ref), custom_call_target="tpu_custom_call" | custom-call | flops 800000000 | bytes 5000000 | tf_op jit(solution)/shard_map/pallas_call | solution.py:282
  (25 shorter events, 0.1 us)
Async XLA Ops:
  6.5 18.6 %copy-start.1 = (f32[128,1024]{1,0:T(8,128)S(1)}, f32[128,1024]{1,0:T(8,128)}, u32[]{:S(2)}) copy-start(f32[128,1024]{1,0:T(8,128)} %basis_ref.1) | copy-start | bytes 1572868
  6.5 47.9 %all-gather.5.cloned.1.call-start = ((), (), s32[]{:S(2)}) async-start(), calls=%async_computation.5 | async-start | bytes 2621440 | tf_op jit(solution)/shard_map/all_gather | solution.py:327
  6.5 9.6 %collective-permute-start = (bf16[128,1024]{1,0:T(8,128)(2,1)}, bf16[128,1024]{1,0:T(8,128)(2,1)S(1)}, u32[]{:S(2)}, u32[]{:S(2)}) collective-permute-start(bf16[128,1024]{1,0:T(8,128)(2,1)} %bitcast.32), channel_id=1, source_target_pairs={{0,16},{16,0},{1,17},{17,1},{2,18},{18,2},{3,19},{19,3},{4,20},{20... | collective-permute-start | bytes 786440 | tf_op jit(solution)/shard_map/ppermute | solution.py:351
  10.4 1.0 copy-start.2
  11.3 0.7 copy-start.3
  12.0 13.1 %copy-start.5 = (f32[128]{0:T(128)S(1)}, f32[128]{0:T(128)}, u32[]{:S(2)}) copy-start(f32[128]{0:T(128)} %param.15) | copy-start | bytes 1540
  15.7 27.7 %copy-start.4 = (f32[1,1024]{1,0:T(1,128)S(1)}, f32[1,1024]{1,0:T(1,128)}, u32[]{:S(2)}) copy-start(f32[1,1024]{1,0:T(1,128)} %values_ref.1) | copy-start | bytes 12292
  18.0 16.0 %all-to-all-start = ((bf16[8,32,512]{2,1,0:T(8,128)(2,1)}), bf16[8,32,512]{2,1,0:T(8,128)(2,1)S(1)}, u32[]{:S(2)}, u32[]{:S(2)}) async-start(bf16[8,32,512]{2,1,0:T(8,128)(2,1)} %shard_map.91), calls=%async_computation | async-start | bytes 524288 | tf_op jit(solution)/shard_map/all_to_all | solution.py:319
  33.9 14.1 %collective-permute-start.4 = (bf16[8,32,512]{2,1,0:T(8,128)(2,1)S(1)}, bf16[8,32,512]{2,1,0:T(8,128)(2,1)S(1)}, u32[]{:S(2)}, u32[]{:S(2)}) collective-permute-start(bf16[8,32,512]{2,1,0:T(8,128)(2,1)S(1)} %all-to-all-done.x0_ref), channel_id=1, source_target_pairs={{0,3},{1,2},{2,1},{3,0},{4,7},{5,6},{6,5},{7,4},{8,11},{9,10},{10,... | collective-permute-start | bytes 786440 | tf_op jit(solution)/shard_map/ppermute | solution.py:320
  33.9 14.1 %collective-permute-start.3 = (bf16[8,32,512]{2,1,0:T(8,128)(2,1)S(1)}, bf16[8,32,512]{2,1,0:T(8,128)(2,1)S(1)}, u32[]{:S(2)}, u32[]{:S(2)}) collective-permute-start(bf16[8,32,512]{2,1,0:T(8,128)(2,1)S(1)} %all-to-all-done.x0_ref), channel_id=1, source_target_pairs={{0,2},{1,3},{2,0},{3,1},{4,6},{5,7},{6,4},{7,5},{8,10},{9,11},{10,... | collective-permute-start | bytes 786440 | tf_op jit(solution)/shard_map/ppermute | solution.py:320
  34.6 13.5 %collective-permute-start.2 = (bf16[8,32,512]{2,1,0:T(8,128)(2,1)S(1)}, bf16[8,32,512]{2,1,0:T(8,128)(2,1)S(1)}, u32[]{:S(2)}, u32[]{:S(2)}) collective-permute-start(bf16[8,32,512]{2,1,0:T(8,128)(2,1)S(1)} %all-to-all-done.x0_ref), channel_id=1, source_target_pairs={{0,1},{1,0},{2,3},{3,2},{4,5},{5,4},{6,7},{7,6},{8,9},{9,8},{10,11... | collective-permute-start | bytes 786440 | tf_op jit(solution)/shard_map/ppermute | solution.py:320
  35.8 6.9 %collective-permute-start.1 = (s32[2,136,128]{2,1,0:T(8,128)S(1)}, s32[2,136,128]{2,1,0:T(8,128)S(1)}, u32[]{:S(2)}, u32[]{:S(2)}) collective-permute-start(s32[2,136,128]{2,1,0:T(8,128)S(1)} %constant_dynamic-slice_fusion.1), channel_id=1, source_target_pairs={{0,18},{2,16},{16,2},{18,0},{1,19},{3,17},{17,3},{19,1},{4,22},{6,... | collective-permute-start | bytes 417800 | tf_op jit(solution)/shard_map/ppermute | solution.py:313
  48.0 38.2 %all-to-all-start.1 = ((s32[32,136,128]{2,1,0:T(8,128)}), s32[32,136,128]{2,1,0:T(8,128)}, u32[]{:S(2)}, u32[]{:S(2)}) async-start(s32[32,136,128]{2,1,0:T(8,128)} %shard_map.92), calls=%async_computation.1 | async-start | bytes 4456448 | tf_op jit(solution)/shard_map/all_to_all | solution.py:324
  54.4 10.2 %copy-start.8 = (s32[32]{0:T(128)S(1)}, s32[32]{0:T(128)}, u32[]{:S(2)}) copy-start(s32[32]{0:T(128)} %param.13) | copy-start | bytes 388
  54.4 88.9 %all-gather.7.cloned.1.call-start = ((), (), s32[]{:S(2)}) async-start(), calls=%async_computation.6 | async-start | bytes 1392640 | tf_op jit(solution)/shard_map/all_gather | solution.py:331
  54.5 1.6 copy-start.6
  58.6 36.0 %collective-permute-start.5 = (s32[520,128]{1,0:T(8,128)S(1)}, s32[520,128]{1,0:T(8,128)S(1)}, u32[]{:S(2)}, u32[]{:S(2)}) collective-permute-start(s32[520,128]{1,0:T(8,128)S(1)} %get-tuple-element.41), channel_id=1, source_target_pairs={{0,4},{4,8},{8,12},{12,0},{1,5},{5,9},{9,13},{13,1},{2,6},{6,10},{... | collective-permute-start | bytes 798728 | tf_op jit(solution)/shard_map/ppermute | solution.py:347
  60.4 34.3 %collective-permute-start.6 = (s32[520,128]{1,0:T(8,128)S(1)}, s32[520,128]{1,0:T(8,128)S(1)}, u32[]{:S(2)}, u32[]{:S(2)}) collective-permute-start(s32[520,128]{1,0:T(8,128)S(1)} %get-tuple-element.42), channel_id=1, source_target_pairs={{0,8},{4,12},{8,0},{12,4},{1,9},{5,13},{9,1},{13,5},{2,10},{6,14},... | collective-permute-start | bytes 798728 | tf_op jit(solution)/shard_map/ppermute | solution.py:347
  63.1 34.4 %collective-permute-start.7 = (s32[520,128]{1,0:T(8,128)S(1)}, s32[520,128]{1,0:T(8,128)S(1)}, u32[]{:S(2)}, u32[]{:S(2)}) collective-permute-start(s32[520,128]{1,0:T(8,128)S(1)} %get-tuple-element.43), channel_id=1, source_target_pairs={{0,12},{4,0},{8,4},{12,8},{1,13},{5,1},{9,5},{13,9},{2,14},{6,2},{... | collective-permute-start | bytes 798728 | tf_op jit(solution)/shard_map/ppermute | solution.py:347
  99.0 52.5 %all-to-all-start.2 = ((s32[32,136,128]{2,1,0:T(8,128)}), s32[32,136,128]{2,1,0:T(8,128)}, u32[]{:S(2)}, u32[]{:S(2)}) async-start(s32[32,136,128]{2,1,0:T(8,128)} %broadcast_in_dim.8), calls=%async_computation.2 | async-start | bytes 4456448 | tf_op jit(solution)/shard_map/all_to_all | solution.py:333
  143.3 4.3 %copy-start = (s32[8,2,136,128]{3,2,1,0:T(8,128)S(1)}, s32[8,2,136,128]{3,2,1,0:T(8,128)}, u32[]{:S(2)}) copy-start(s32[8,2,136,128]{3,2,1,0:T(8,128)} %all-gather.7.cloned.1.call-done) | copy-start | bytes 3342340
  144.7 1.6 collective-permute-start.8
  144.8 1.9 collective-permute-start.11
  145.3 1.8 collective-permute-start.10
  145.4 2.1 %collective-permute-start.9 = (s32[2,2,136,128]{3,2,1,0:T(8,128)S(1)}, s32[2,2,136,128]{3,2,1,0:T(8,128)S(1)}, u32[]{:S(2)}, u32[]{:S(2)}) collective-permute-start(s32[2,2,136,128]{3,2,1,0:T(8,128)S(1)} %get-tuple-element.62), channel_id=1, source_target_pairs={{0,1},{1,0},{2,3},{3,2},{4,5},{5,4},{6,7},{7,6},{8,9},{9,8},{10,11... | collective-permute-start | bytes 835592 | tf_op jit(solution)/shard_map/ppermute | solution.py:351
  151.5 21.8 %copy-start.7 = (bf16[1024,1024]{1,0:T(8,128)(2,1)S(1)}, bf16[1024,1024]{1,0:T(8,128)(2,1)}, u32[]{:S(2)}) copy-start(bf16[1024,1024]{1,0:T(8,128)(2,1)} %get-tuple-element.55.low_ref) | copy-start | bytes 6291460
Sparse Core Ops, SparseCore 0:
  18.1 33.4 all-gather.4
  97.6 45.6 all-gather.6

commit v3 on v1

--- a/solution.py
+++ b/solution.py
@@ -329,7 +329,7 @@
     in_all = lax.all_gather(in_pair, "z")
     own, *words = partial_rows(me, tokens, grads)
     words = [along(w, "z", k + 1) for k, w in enumerate(words)]
-    piece, words = lax.optimization_barrier((piece, words))
+    piece, words[0], words[2] = lax.optimization_barrier((piece, words[0], words[2]))
 
     got = lax.all_to_all(jnp.broadcast_to(piece, spread.shape), ALL_DP, 0, 0, tiled=True)
     in_high, in_low, in_side = unpack_basis(me, in_all, jnp.stack([flip(in_all[z], "c") for z in range(4)]))

time: 190 us -> 185 us (0.974)
  waiting for transfers between devices: 80.1 us -> 73.5 us
  starting transfers between devices: 31.5 us -> 35.5 us
  blocking collectives: 28.7 us -> 26.2 us
    all_to_all x1, waiting for transfers between devices: 22.4 us -> 0.01 us  [body(): lax.all_to_all(jnp.broadcast_to(piece, spread.shape), ALL_DP, 0, 0, tiled...]
    ppermute x3, waiting for transfers between devices: 19.3 us -> 34.7 us  [along(): return lax.ppermute(block, axis, [(i, (i + shift) % 4) for i in range(4)])]
    all_to_all x1, starting transfers between devices: 5.24 us -> 8.73 us  [body(): lax.all_to_all(jnp.broadcast_to(piece, spread.shape), ALL_DP, 0, 0, tiled...]
    all_to_all x1, waiting for transfers between devices: 21.5 us -> 23.7 us  [body(): spread = lax.all_to_all(packed, ALL_DP, 0, 0, tiled=True)]
    all_to_all x1, blocking collectives: 15.4 us -> 13.3 us  [body(): v = lax.all_to_all(v, PAIR, 0, 0, tiled=True)]
  transfers between devices with their start and end apart: 17 -> 17, of which waited for: 12 -> 6; matrix products, arithmetic and copies ran while one was open for 3% -> 3% of each run, Pallas kernels for 8% -> 8%
where the time goes in v3:
time: 185 us
  waiting for transfers between devices  73.5 us (40%)
  starting transfers between devices  35.5 us (19%)
  blocking collectives  26.2 us (14%)
  Pallas kernels  25.3 us (14%)
  between operations  13.7 us (7%)
  local copies, waits for them, and re-layouts  7.83 us (4%)
  other arithmetic  2.6 us (1%)
    ppermute x3, waiting for transfers between devices, along(): return lax.ppermute(block, axis, [(i, (i + shift) % 4) for i in range(4)])  34.7 us
    all_to_all x1, waiting for transfers between devices, body(): spread = lax.all_to_all(packed, ALL_DP, 0, 0, tiled=True)  23.7 us
    all_to_all x1, blocking collectives, body(): v = lax.all_to_all(v, PAIR, 0, 0, tiled=True)  13.3 us
    all_to_all x1, blocking collectives, body(): u = lax.all_to_all(u, PAIR, 0, 0, tiled=True)  12.8 us
    all_to_all x1, starting transfers between devices, body(): lax.all_to_all(jnp.broadcast_to(piece, spread.shape), ALL_DP, 0, 0, tiled...  8.73 us
    all_to_all x1, waiting for transfers between devices, body(): moved = lax.all_to_all(chunks, ('y', 'h'), 0, 0, tiled=True)  8.41 us
    all_to_all x1, starting transfers between devices, body(): moved = lax.all_to_all(chunks, ('y', 'h'), 0, 0, tiled=True)  7.17 us
    ppermute x3, starting transfers between devices, along(): return lax.ppermute(block, axis, [(i, (i + shift) % 4) for i in range(4)])  6.47 us
  transfers between devices with their start and end apart: 17, of which 6 were waited for; matrix products, arithmetic and copies ran while one was open for 3% of the time, Pallas kernels for 8%

profile of v3, /device:TPU:0, one launch (start us, length us, event | category | flops | bytes accessed | tf_op | source)
XLA Modules:
  0.0 184.6 jit_solution(3493925693003706651)
XLA Ops:
  6.5 3.1 %collective-permute-start = (bf16[128,1024]{1,0:T(8,128)(2,1)}, bf16[128,1024]{1,0:T(8,128)(2,1)S(1)}, u32[]{:S(2)}, u32[]{:S(2)}) collective-permute-start(bf16[128,1024]{1,0:T(8,128)(2,1)} %bitcast.32), channel_id=1, source_target_pairs={{0,16},{16,0},{1,17},{17,1},{2,18},{18,2},{3,19},{19,3},{4,20},{20... | collective-permute-start | bytes 786440 | tf_op jit(solution)/shard_map/ppermute | solution.py:352
  9.6 0.7 concatenate.3.me_ref
  10.4 0.9 copy-done.2
  11.3 0.7 copy-done.3
  12.1 3.6 %shard_map.91 = bf16[8,32,512]{2,1,0:T(8,128)(2,1)} custom-call(s32[8]{0:T(128)S(1)} %concatenate.3.me_ref, s32[1,4096]{1,0:T(1,128)S(1)} %copy-done.3, bf16[32,4096]{1,0:T(8,128)(2,1)S(1)} %bitcast.24), custom_call_target="tpu_custom_call" | custom-call | flops 1000000 | bytes 1000000 | tf_op jit(solution)/shard_map/pallas_call | solution.py:52
  15.7 0.5 collective-permute-done
  16.2 1.8 pad_maximum_fusion
  18.0 0.0 all-gather.5.cloned.1.call-update
  18.0 7.2 %all-to-all-start = ((bf16[8,32,512]{2,1,0:T(8,128)(2,1)}), bf16[8,32,512]{2,1,0:T(8,128)(2,1)S(1)}, u32[]{:S(2)}, u32[]{:S(2)}) async-start(bf16[8,32,512]{2,1,0:T(8,128)(2,1)} %shard_map.91), calls=%async_computation | async-start | bytes 524288 | tf_op jit(solution)/shard_map/all_to_all | solution.py:319
  25.2 0.4 shard_map.93
  25.5 8.4 %all-to-all-done.x0_ref = bf16[8,32,512]{2,1,0:T(8,128)(2,1)S(1)} async-done(((bf16[8,32,512]{2,1,0:T(8,128)(2,1)}), bf16[8,32,512]{2,1,0:T(8,128)(2,1)S(1)}, u32[]{:S(2)}, u32[]{:S(2)}) %all-to-all-start) | async-done | bytes 262176 | tf_op jit(solution)/shard_map/all_to_all | solution.py:319
  33.9 0.6 collective-permute-start.3
  34.6 1.2 collective-permute-start.2
  35.8 0.7 collective-permute-start.1
  36.5 6.2 %collective-permute-done.1 = s32[2,136,128]{2,1,0:T(8,128)S(1)} collective-permute-done((s32[2,136,128]{2,1,0:T(8,128)S(1)}, s32[2,136,128]{2,1,0:T(8,128)S(1)}, u32[]{:S(2)}, u32[]{:S(2)}) %collective-permute-start.1) | collective-permute-done | bytes 139296 | tf_op jit(solution)/shard_map/ppermute | solution.py:313
  42.7 0.7 pad_add_fusion.1
  43.4 4.6 %shard_map.92 = s32[32,136,128]{2,1,0:T(8,128)} custom-call(f32[1024,1024]{1,0:T(8,128)} %bitcast.27, f32[1,1024]{1,0:T(1,128)S(1)} %copy-done.4), custom_call_target="tpu_custom_call" | custom-call | flops 10240000 | bytes 6144000 | tf_op jit(solution)/shard_map/pallas_call | solution.py:113
  48.0 0.0 collective-permute-done.4.x3_ref
  48.0 0.0 collective-permute-done.3.x2_ref
  48.0 6.4 %all-to-all-start.1 = ((s32[32,136,128]{2,1,0:T(8,128)}), s32[32,136,128]{2,1,0:T(8,128)}, u32[]{:S(2)}, u32[]{:S(2)}) async-start(s32[32,136,128]{2,1,0:T(8,128)} %shard_map.92), calls=%async_computation.1 | async-start | bytes 4456448 | tf_op jit(solution)/shard_map/all_to_all | solution.py:324
  54.4 0.0 copy-start.8
  54.4 0.0 all-gather.7.cloned.1.call-start
  54.4 0.0 all-gather.5.cloned.1.call-done
  54.5 1.6 copy-done.6
  56.1 3.1 %shard_map.94 = (f32[128,1024]{1,0:T(8,128)S(1)}, s32[520,128]{1,0:T(8,128)S(1)}, s32[520,128]{1,0:T(8,128)}, s32[520,128]{1,0:T(8,128)S(1)}) custom-call(s32[8]{0:T(128)S(1)} %concatenate.3.me_ref, bf16[8,32,512]{2,1,0:T(8,128)(2,1)S(1)} %all-to-all-done.x0_ref, bf16[8,32,512]{2,1,0:T(8,128)(2,1)S(1)} %collective-permute-done.2.x1_ref, ...), custom_call_target="tpu_custom_call" | custom-call | flops 1000000000 | bytes 5000000 | tf_op jit(solution)/shard_map/pallas_call | solution.py:190
  59.2 1.7 collective-permute-start.5
  60.9 1.5 collective-permute-start.6
  62.4 0.0 all-gather.7.cloned.1.call-update
  62.5 23.7 %all-to-all-done.1 = s32[32,136,128]{2,1,0:T(8,128)} async-done(((s32[32,136,128]{2,1,0:T(8,128)}), s32[32,136,128]{2,1,0:T(8,128)}, u32[]{:S(2)}, u32[]{:S(2)}) %all-to-all-start.1) | async-done | bytes 2228256 | tf_op jit(solution)/shard_map/all_to_all | solution.py:324
  86.2 0.9 constant_dynamic-slice_fusion.out_side_ref
  87.1 7.2 %collective-permute-done.5.w1_ref = s32[520,128]{1,0:T(8,128)S(1)} collective-permute-done((s32[520,128]{1,0:T(8,128)S(1)}, s32[520,128]{1,0:T(8,128)S(1)}, u32[]{:S(2)}, u32[]{:S(2)}) %collective-permute-start.5) | collective-permute-done | bytes 266272 | tf_op jit(solution)/shard_map/ppermute | solution.py:348
  94.3 1.5 broadcast_in_dim.8
  95.8 8.7 %all-to-all-start.2 = ((s32[32,136,128]{2,1,0:T(8,128)}), s32[32,136,128]{2,1,0:T(8,128)}, u32[]{:S(2)}, u32[]{:S(2)}) async-start(s32[32,136,128]{2,1,0:T(8,128)} %broadcast_in_dim.8), calls=%async_computation.2 | async-start | bytes 4456448 | tf_op jit(solution)/shard_map/all_to_all | solution.py:334
  104.5 0.0 all-gather.7.cloned.1.call-done
  104.6 1.4 fusion
  106.0 0.1 collective-permute-start.7
  106.1 0.5 collective-permute-start.10
  106.6 0.1 collective-permute-start.9
  106.7 0.4 collective-permute-start.8
  107.1 3.2 %collective-permute-start.11 = (s32[520,128]{1,0:T(8,128)}, s32[520,128]{1,0:T(8,128)S(1)}, u32[]{:S(2)}, u32[]{:S(2)}) collective-permute-start(s32[520,128]{1,0:T(8,128)} %get-tuple-element.49), channel_id=1, source_target_pairs={{0,8},{4,12},{8,0},{12,4},{1,9},{5,13},{9,1},{13,5},{2,10},{6,14},... | collective-permute-start | bytes 798728 | tf_op jit(solution)/shard_map/ppermute | solution.py:348
  110.3 0.1 pad_add_fusion.other_ref
  110.4 3.9 %shard_map.95 = (bf16[1024,1024]{1,0:T(8,128)(2,1)S(1)}, bf16[1024,1024]{1,0:T(8,128)(2,1)}, s32[8,8,128]{2,1,0:T(8,128)S(1)}) custom-call(s32[8]{0:T(128)S(1)} %concatenate.3.me_ref, s32[4,2,2,136,128]{4,3,2,1,0:T(8,128)S(1)} %bitcast.22, s32[4,2,2,136,128]{4,3,2,1,0:T(8,128)S(1)} %pad_add_fusion.other_ref), custom_call_target="tpu_custom_call" | custom-call | flops 10000000 | bytes 6000000 | tf_op jit(solution)/shard_map/pallas_call | solution.py:150
  114.3 27.5 %collective-permute-done.11.w2_ref = s32[520,128]{1,0:T(8,128)S(1)} collective-permute-done((s32[520,128]{1,0:T(8,128)}, s32[520,128]{1,0:T(8,128)S(1)}, u32[]{:S(2)}, u32[]{:S(2)}) %collective-permute-start.11) | collective-permute-done | bytes 266272 | tf_op jit(solution)/shard_map/ppermute | solution.py:348
  141.8 5.2 %shard_map.96 = (f32[8,128,128]{2,1,0:T(8,128)S(1)}, bf16[1024,1024]{1,0:T(8,128)(2,1)S(1)}, bf16[1024,1024]{1,0:T(8,128)(2,1)S(1)}) custom-call(s32[32,136,128]{2,1,0:T(8,128)} %all-to-all-done.2.got_ref, f32[128,1024]{1,0:T(8,128)S(1)} %get-tuple-element.47.own_ref, s32[520,128]{1,0:T(8,128)S(1)} %collective-permute-done.5.w1_ref, ...), custom_call_target="tpu_custom_call" | custom-call | flops 800000000 | bytes 8000000 | tf_op jit(solution)/shard_map/pallas_call | solution.py:226
  147.1 13.3 %all_to_all.25.v_ref = f32[8,128,128]{2,1,0:T(8,128)S(1)} all-to-all(f32[8,128,128]{2,1,0:T(8,128)S(1)} %get-tuple-element.51), channel_id=1, replica_groups=mesh['y'=4,'h'=2,'z'=4,'l'=2,'c'=2] {'h','z'}, dimensions={0} | all-to-all | bytes 1048576 | tf_op jit(solution)/shard_map/all_to_all | solution.py:339
  160.4 2.3 %shard_map.97 = f32[8,128,128]{2,1,0:T(8,128)S(1)} custom-call(f32[8,128,128]{2,1,0:T(8,128)S(1)} %all_to_all.25.v_ref, bf16[1024,1024]{1,0:T(8,128)(2,1)S(1)} %get-tuple-element.52.high_ref, bf16[1024,1024]{1,0:T(8,128)(2,1)S(1)} %copy-done.7, s32[8,8,128]{2,1,0:T(8,128)S(1)} %get-tuple-element.54.in_side_ref, ...), custom_call_target="tpu_custom_call" | custom-call | flops 1600000000 | bytes 6000000 | tf_op jit(solution)/shard_map/pallas_call | solution.py:258
  162.7 12.8 %all_to_all.26.u_ref = f32[8,128,128]{2,1,0:T(8,128)S(1)} all-to-all(f32[8,128,128]{2,1,0:T(8,128)S(1)} %shard_map.97), channel_id=1, replica_groups=mesh['y'=4,'h'=2,'z'=4,'l'=2,'c'=2] {'h','z'}, dimensions={0} | all-to-all | bytes 1048576 | tf_op jit(solution)/shard_map/all_to_all | solution.py:341
  175.5 2.2 %shard_map.98 = f32[128,1024]{1,0:T(8,128)} custom-call(f32[8,128,128]{2,1,0:T(8,128)S(1)} %all_to_all.26.u_ref, bf16[1024,1024]{1,0:T(8,128)(2,1)S(1)} %get-tuple-element.55.high_ref, bf16[1024,1024]{1,0:T(8,128)(2,1)S(1)} %get-tuple-element.56.low_ref), custom_call_target="tpu_custom_call" | custom-call | flops 800000000 | bytes 5000000 | tf_op jit(solution)/shard_map/pallas_call | solution.py:282
  (25 shorter events, 0.1 us)
Async XLA Ops:
  6.5 18.6 %copy-start.1 = (f32[128,1024]{1,0:T(8,128)S(1)}, f32[128,1024]{1,0:T(8,128)}, u32[]{:S(2)}) copy-start(f32[128,1024]{1,0:T(8,128)} %basis_ref.1) | copy-start | bytes 1572868
  6.5 47.9 %all-gather.5.cloned.1.call-start = ((), (), s32[]{:S(2)}) async-start(), calls=%async_computation.5 | async-start | bytes 2621440 | tf_op jit(solution)/shard_map/all_gather | solution.py:327
  6.5 9.6 %collective-permute-start = (bf16[128,1024]{1,0:T(8,128)(2,1)}, bf16[128,1024]{1,0:T(8,128)(2,1)S(1)}, u32[]{:S(2)}, u32[]{:S(2)}) collective-permute-start(bf16[128,1024]{1,0:T(8,128)(2,1)} %bitcast.32), channel_id=1, source_target_pairs={{0,16},{16,0},{1,17},{17,1},{2,18},{18,2},{3,19},{19,3},{4,20},{20... | collective-permute-start | bytes 786440 | tf_op jit(solution)/shard_map/ppermute | solution.py:352
  10.4 1.0 copy-start.2
  11.3 0.7 copy-start.3
  12.0 13.1 %copy-start.5 = (f32[128]{0:T(128)S(1)}, f32[128]{0:T(128)}, u32[]{:S(2)}) copy-start(f32[128]{0:T(128)} %param.15) | copy-start | bytes 1540
  15.7 27.7 %copy-start.4 = (f32[1,1024]{1,0:T(1,128)S(1)}, f32[1,1024]{1,0:T(1,128)}, u32[]{:S(2)}) copy-start(f32[1,1024]{1,0:T(1,128)} %values_ref.1) | copy-start | bytes 12292
  18.0 16.0 %all-to-all-start = ((bf16[8,32,512]{2,1,0:T(8,128)(2,1)}), bf16[8,32,512]{2,1,0:T(8,128)(2,1)S(1)}, u32[]{:S(2)}, u32[]{:S(2)}) async-start(bf16[8,32,512]{2,1,0:T(8,128)(2,1)} %shard_map.91), calls=%async_computation | async-start | bytes 524288 | tf_op jit(solution)/shard_map/all_to_all | solution.py:319
  33.9 14.1 %collective-permute-start.4 = (bf16[8,32,512]{2,1,0:T(8,128)(2,1)S(1)}, bf16[8,32,512]{2,1,0:T(8,128)(2,1)S(1)}, u32[]{:S(2)}, u32[]{:S(2)}) collective-permute-start(bf16[8,32,512]{2,1,0:T(8,128)(2,1)S(1)} %all-to-all-done.x0_ref), channel_id=1, source_target_pairs={{0,3},{1,2},{2,1},{3,0},{4,7},{5,6},{6,5},{7,4},{8,11},{9,10},{10,... | collective-permute-start | bytes 786440 | tf_op jit(solution)/shard_map/ppermute | solution.py:320
  33.9 14.1 %collective-permute-start.3 = (bf16[8,32,512]{2,1,0:T(8,128)(2,1)S(1)}, bf16[8,32,512]{2,1,0:T(8,128)(2,1)S(1)}, u32[]{:S(2)}, u32[]{:S(2)}) collective-permute-start(bf16[8,32,512]{2,1,0:T(8,128)(2,1)S(1)} %all-to-all-done.x0_ref), channel_id=1, source_target_pairs={{0,2},{1,3},{2,0},{3,1},{4,6},{5,7},{6,4},{7,5},{8,10},{9,11},{10,... | collective-permute-start | bytes 786440 | tf_op jit(solution)/shard_map/ppermute | solution.py:320
  34.6 13.5 %collective-permute-start.2 = (bf16[8,32,512]{2,1,0:T(8,128)(2,1)S(1)}, bf16[8,32,512]{2,1,0:T(8,128)(2,1)S(1)}, u32[]{:S(2)}, u32[]{:S(2)}) collective-permute-start(bf16[8,32,512]{2,1,0:T(8,128)(2,1)S(1)} %all-to-all-done.x0_ref), channel_id=1, source_target_pairs={{0,1},{1,0},{2,3},{3,2},{4,5},{5,4},{6,7},{7,6},{8,9},{9,8},{10,11... | collective-permute-start | bytes 786440 | tf_op jit(solution)/shard_map/ppermute | solution.py:320
  35.8 6.9 %collective-permute-start.1 = (s32[2,136,128]{2,1,0:T(8,128)S(1)}, s32[2,136,128]{2,1,0:T(8,128)S(1)}, u32[]{:S(2)}, u32[]{:S(2)}) collective-permute-start(s32[2,136,128]{2,1,0:T(8,128)S(1)} %constant_dynamic-slice_fusion.1), channel_id=1, source_target_pairs={{0,18},{2,16},{16,2},{18,0},{1,19},{3,17},{17,3},{19,1},{4,22},{6,... | collective-permute-start | bytes 417800 | tf_op jit(solution)/shard_map/ppermute | solution.py:313
  48.0 38.2 %all-to-all-start.1 = ((s32[32,136,128]{2,1,0:T(8,128)}), s32[32,136,128]{2,1,0:T(8,128)}, u32[]{:S(2)}, u32[]{:S(2)}) async-start(s32[32,136,128]{2,1,0:T(8,128)} %shard_map.92), calls=%async_computation.1 | async-start | bytes 4456448 | tf_op jit(solution)/shard_map/all_to_all | solution.py:324
  54.4 8.1 %copy-start.8 = (s32[32]{0:T(128)S(1)}, s32[32]{0:T(128)}, u32[]{:S(2)}) copy-start(s32[32]{0:T(128)} %param.13) | copy-start | bytes 388
  54.4 50.2 %all-gather.7.cloned.1.call-start = ((), (), s32[]{:S(2)}) async-start(), calls=%async_computation.6 | async-start | bytes 1392640 | tf_op jit(solution)/shard_map/all_gather | solution.py:329
  54.5 1.6 copy-start.6
  59.2 35.1 %collective-permute-start.5 = (s32[520,128]{1,0:T(8,128)S(1)}, s32[520,128]{1,0:T(8,128)S(1)}, u32[]{:S(2)}, u32[]{:S(2)}) collective-permute-start(s32[520,128]{1,0:T(8,128)S(1)} %get-tuple-element.39), channel_id=1, source_target_pairs={{0,4},{4,8},{8,12},{12,0},{1,5},{5,9},{9,13},{13,1},{2,6},{6,10},{... | collective-permute-start | bytes 798728 | tf_op jit(solution)/shard_map/ppermute | solution.py:348
  60.9 33.4 %collective-permute-start.6 = (s32[520,128]{1,0:T(8,128)S(1)}, s32[520,128]{1,0:T(8,128)S(1)}, u32[]{:S(2)}, u32[]{:S(2)}) collective-permute-start(s32[520,128]{1,0:T(8,128)S(1)} %get-tuple-element.40), channel_id=1, source_target_pairs={{0,12},{4,0},{8,4},{12,8},{1,13},{5,1},{9,5},{13,9},{2,14},{6,2},{... | collective-permute-start | bytes 798728 | tf_op jit(solution)/shard_map/ppermute | solution.py:348
  95.8 46.0 %all-to-all-start.2 = ((s32[32,136,128]{2,1,0:T(8,128)}), s32[32,136,128]{2,1,0:T(8,128)}, u32[]{:S(2)}, u32[]{:S(2)}) async-start(s32[32,136,128]{2,1,0:T(8,128)} %broadcast_in_dim.8), calls=%async_computation.2 | async-start | bytes 4456448 | tf_op jit(solution)/shard_map/all_to_all | solution.py:334
  104.6 5.8 %copy-start = (s32[8,2,136,128]{3,2,1,0:T(8,128)S(1)}, s32[8,2,136,128]{3,2,1,0:T(8,128)}, u32[]{:S(2)}) copy-start(s32[8,2,136,128]{3,2,1,0:T(8,128)} %all-gather.7.cloned.1.call-done) | copy-start | bytes 3342340
  106.0 4.3 %collective-permute-start.7 = (s32[2,2,136,128]{3,2,1,0:T(8,128)S(1)}, s32[2,2,136,128]{3,2,1,0:T(8,128)S(1)}, u32[]{:S(2)}, u32[]{:S(2)}) collective-permute-start(s32[2,2,136,128]{3,2,1,0:T(8,128)S(1)} %get-tuple-element.57), channel_id=1, source_target_pairs={{0,1},{1,0},{2,3},{3,2},{4,5},{5,4},{6,7},{7,6},{8,9},{9,8},{10,11... | collective-permute-start | bytes 835592 | tf_op jit(solution)/shard_map/ppermute | solution.py:352
  106.1 4.2 %collective-permute-start.10 = (s32[2,2,136,128]{3,2,1,0:T(8,128)S(1)}, s32[2,2,136,128]{3,2,1,0:T(8,128)S(1)}, u32[]{:S(2)}, u32[]{:S(2)}) collective-permute-start(s32[2,2,136,128]{3,2,1,0:T(8,128)S(1)} %get-tuple-element.58), channel_id=1, source_target_pairs={{0,1},{1,0},{2,3},{3,2},{4,5},{5,4},{6,7},{7,6},{8,9},{9,8},{10,11... | collective-permute-start | bytes 835592 | tf_op jit(solution)/shard_map/ppermute | solution.py:352
  106.6 3.8 %collective-permute-start.9 = (s32[2,2,136,128]{3,2,1,0:T(8,128)S(1)}, s32[2,2,136,128]{3,2,1,0:T(8,128)S(1)}, u32[]{:S(2)}, u32[]{:S(2)}) collective-permute-start(s32[2,2,136,128]{3,2,1,0:T(8,128)S(1)} %get-tuple-element.59), channel_id=1, source_target_pairs={{0,1},{1,0},{2,3},{3,2},{4,5},{5,4},{6,7},{7,6},{8,9},{9,8},{10,11... | collective-permute-start | bytes 835592 | tf_op jit(solution)/shard_map/ppermute | solution.py:352
  106.7 3.7 %collective-permute-start.8 = (s32[2,2,136,128]{3,2,1,0:T(8,128)S(1)}, s32[2,2,136,128]{3,2,1,0:T(8,128)S(1)}, u32[]{:S(2)}, u32[]{:S(2)}) collective-permute-start(s32[2,2,136,128]{3,2,1,0:T(8,128)S(1)} %get-tuple-element.60), channel_id=1, source_target_pairs={{0,1},{1,0},{2,3},{3,2},{4,5},{5,4},{6,7},{7,6},{8,9},{9,8},{10,11... | collective-permute-start | bytes 835592 | tf_op jit(solution)/shard_map/ppermute | solution.py:352
  107.1 34.8 %collective-permute-start.11 = (s32[520,128]{1,0:T(8,128)}, s32[520,128]{1,0:T(8,128)S(1)}, u32[]{:S(2)}, u32[]{:S(2)}) collective-permute-start(s32[520,128]{1,0:T(8,128)} %get-tuple-element.49), channel_id=1, source_target_pairs={{0,8},{4,12},{8,0},{12,4},{1,9},{5,13},{9,1},{13,5},{2,10},{6,14},... | collective-permute-start | bytes 798728 | tf_op jit(solution)/shard_map/ppermute | solution.py:348
  141.8 18.6 %copy-start.7 = (bf16[1024,1024]{1,0:T(8,128)(2,1)S(1)}, bf16[1024,1024]{1,0:T(8,128)(2,1)}, u32[]{:S(2)}) copy-start(bf16[1024,1024]{1,0:T(8,128)(2,1)} %get-tuple-element.53.low_ref) | copy-start | bytes 6291460
Sparse Core Ops, SparseCore 0:
  18.1 33.4 all-gather.4
  62.5 35.8 all-gather.6
